TPU v7x, 256 devices: a whole 4x4x8 slice. The times are simulated.
256 devices in a mesh: front: 4 (over x), row: 4 (over y), col: 16 (over z, core).
Axes of the slice: x: 4, y: 4, z: 8, core: 2. Of those that a mesh axis runs over, the one named last changes fastest.
Arguments:
- child_rhs: float32 [4, 8192, 128], P('front', 'col'), may hold values from -6 to 6
- root_rhs: float32 [12288, 128], P('col'), may hold values from -6 to 6
- child_inv: float32 [4, 8192, 8192], P('front', 'row', 'col'), may hold values from -0.0625 to 0.0625
- coupling: float32 [4, 8192, 6144], P('front', 'row', 'col'), may hold values from -0.0625 to 0.0625
- root_inv: float32 [12288, 12288], P(('front', 'row'), 'col'), may hold values from -0.0546875 to 0.0546875
- pivot_counts: int32 [4], replicated, may hold values from 4096 to 8192, as said below
- border_map: int32 [4, 6144], P('front', 'col'), may hold values from 0 to 12287, as said below
Outputs:
- child_solution: float32 [4, 8192, 128], P('front', 'col')
- root_solution: float32 [12288, 128], P('col')
Inputs may be any that keep to these rules, and one draw needn't show every extreme that they name: `pivot_counts`: each child front has 4096 to 8192 live pivots; some front has exactly 8192 in every draw. `border_map`: border rows of one front map to distinct root rows; the k-th of 16 equal blocks of border rows maps into the k-th of 16 equal blocks of root rows.
All inputs are finite; a program needn't handle non-finite values.
Results may differ from a plain program's by a relative error of at most 0.0001.
Values sent between devices are 32-bit elements; how exact they have to be, the bound alone decides.
A program may use at most 64 MiB of HBM per device.

v0:
```python
import jax
import jax.numpy as jnp
from jax import lax
from jax.sharding import PartitionSpec as P

HIGH = lax.Precision.HIGHEST


def lead_dot(left, right):
    return lax.dot_general(left, right, (((0,), (0,)), ((), ())), precision=HIGH)


def per_device(child_rhs, root_rhs, child_inv, coupling, root_inv, pivot_counts, border_map):
    front_index = lax.axis_index("front")
    row_index = lax.axis_index("row")
    col_index = lax.axis_index("col")
    inverse = child_inv[0]
    couple = coupling[0]
    mapping = border_map[0]
    count = jnp.sum(jnp.where(jnp.arange(pivot_counts.shape[0]) == front_index, pivot_counts, 0))
    row_span = inverse.shape[0]
    col_span = inverse.shape[1]
    row_live = (row_index * row_span + jnp.arange(row_span) < count).astype(jnp.float32)[:, None]
    col_live = (col_index * col_span + jnp.arange(col_span) < count).astype(jnp.float32)[:, None]
    root_span = root_rhs.shape[0]
    placed = (mapping[:, None] - col_index * root_span == jnp.arange(root_span)[None, :]).astype(
        jnp.float32
    )
    rhs = child_rhs[0]
    masked = col_live * rhs
    forward = lax.psum(jnp.dot(inverse, masked, precision=HIGH), "col")
    forward = row_live * forward
    border = lead_dot(couple, forward)
    spread = lead_dot(placed, border)
    update = root_rhs - lax.psum(spread, ("front", "row"))
    root_fwd = lax.psum(jnp.dot(root_inv, update, precision=HIGH), "col")
    root_back = lax.psum(lead_dot(root_inv, root_fwd), ("front", "row"))
    picked = jnp.dot(placed, root_back, precision=HIGH)
    correction = lax.psum(jnp.dot(couple, picked, precision=HIGH), "col")
    reduced = row_live * (forward - correction)
    child_back = col_live * lax.psum(lead_dot(inverse, reduced), "row")
    return (child_back[None], root_back)


def solution(mesh):
    in_specs = (
        P("front", "col", None),
        P("col", None),
        P("front", "row", "col"),
        P("front", "row", "col"),
        P(("front", "row"), "col"),
        P(),
        P("front", "col"),
    )
    out_specs = (P("front", "col", None), P("col", None))
    return jax.shard_map(
        per_device, mesh=mesh, in_specs=in_specs, out_specs=out_specs, check_vma=False
    )
```

profile of v0, /device:TPU:1, one launch (start us, length us, event | category | flops | bytes accessed | tf_op | source)
XLA Modules:
  0.0 621.7 jit_solution(1961871332682350369)
XLA Ops:
  7.2 1.4 fusion.35
  8.7 0.6 fusion.34
  9.3 7.8 %fusion.11 = f32[2048,128]{0,1:T(8,128)} fusion(f32[1,2048,512]{2,1,0:T(8,128)} %param.9, f32[1,512,128]{2,1,0:T(8,128)} %param.7, f32[512]{0:T(512)S(1)} %fusion.34), kind=kOutput, calls=%fused_computation.9 | convolution fusion | flops 1610678272 | bytes 5507072 | tf_op jit(solution)/shard_map/dot_general | solution.py:31
  17.1 0.0 all-reduce.9.cloned.1.call-start
  17.2 0.7 fusion.33
  17.9 114.4 %all-reduce.7.cloned.1.call-done = f32[2048,128]{0,1:T(8,128)} async-done(((f32[2048,128]{0,1:T(8,128)}), f32[2048,128]{0,1:T(8,128)}) %all-reduce.7.cloned.1.call-update) | async-done | bytes 1048592 | tf_op jit(solution)/shard_map/psum | solution.py:31
  132.3 3.4 fusion.6
  135.7 1.7 fusion.23
  137.4 0.0 all-reduce.11.cloned.1.call-start
  137.5 93.6 %all-reduce.9.cloned.1.call-done = f32[768,128]{1,0:T(8,128)} async-done(((f32[768,128]{1,0:T(8,128)}), f32[768,128]{1,0:T(8,128)}) %all-reduce.9.cloned.1.call-update) | async-done | bytes 393232 | tf_op jit(solution)/shard_map/psum | solution.py:35
  231.1 4.7 convolution_bitcast_fusion.1
  235.7 0.0 all-reduce.13.cloned.1.call-start
  235.8 110.1 %all-reduce.11.cloned.1.call-done = f32[768,128]{0,1:T(8,128)} async-done(((f32[768,128]{0,1:T(8,128)}), f32[768,128]{0,1:T(8,128)}) %all-reduce.11.cloned.1.call-update) | async-done | bytes 393232 | tf_op jit(solution)/shard_map/psum | solution.py:36
  345.9 4.0 convolution_bitcast_fusion
  349.9 0.2 all-reduce.15.cloned.1.call-start
  350.1 93.4 %all-reduce.13.cloned.1.call-done = f32[768,128]{0,1:T(8,128)} async-done(((f32[768,128]{0,1:T(8,128)}), f32[768,128]{0,1:T(8,128)}) %all-reduce.13.cloned.1.call-update) | async-done | bytes 393232 | tf_op jit(solution)/shard_map/psum | solution.py:37
  443.5 1.7 fusion.14
  445.2 4.4 fusion.8
  449.7 112.0 %all-reduce.15.cloned.1.call-done = f32[2048,128]{0,1:T(8,128)} async-done(((f32[2048,128]{0,1:T(8,128)}), f32[2048,128]{0,1:T(8,128)}) %all-reduce.15.cloned.1.call-update) | async-done | bytes 1048592 | tf_op jit(solution)/shard_map/psum | solution.py:39
  561.7 6.0 fusion.16
  567.8 0.9 copy.10
  568.7 44.3 %all-reduce.17.cloned.1.call-done = f32[512,128]{0,1:T(8,128)} async-done(((f32[512,128]{0,1:T(8,128)}), f32[512,128]{0,1:T(8,128)}) %all-reduce.17.cloned.1.call-update) | async-done | bytes 262160 | tf_op jit(solution)/shard_map/psum | solution.py:41
  613.0 1.0 multiply_bitcast_fusion
  614.0 0.8 copy.9
  (17 shorter events, 0.2 us)
Async XLA Ops:
  7.2 125.1 %copy-start = (f32[1,2048,384]{2,1,0:T(8,128)S(1)}, f32[1,2048,384]{2,1,0:T(8,128)}, u32[]{:S(2)}) copy-start(f32[1,2048,384]{2,1,0:T(8,128)} %param.10) | copy-start | bytes 9437188
  7.2 125.1 %all-reduce.7.cloned.1.call-start = ((), (), s32[]{:S(2)}) async-start(), calls=%async_computation | async-start | bytes 2097152 | tf_op jit(solution)/shard_map/psum | solution.py:31
  9.3 7.8 %copy-start.3 = (s32[1,384]{1,0:T(1,128)S(1)}, s32[1,384]{1,0:T(1,128)}, u32[]{:S(2)}) copy-start(s32[1,384]{1,0:T(1,128)} %param.13) | copy-start | bytes 4612
  17.1 214.0 %copy-start.2 = (f32[768,128]{1,0:T(8,128)S(1)}, f32[768,128]{1,0:T(8,128)}, u32[]{:S(2)}) copy-start(f32[768,128]{1,0:T(8,128)} %param.8) | copy-start | bytes 1179652
  17.1 213.9 %all-reduce.9.cloned.1.call-start = ((), (), s32[]{:S(2)}) async-start(), calls=%async_computation.1 | async-start | bytes 786432 | tf_op jit(solution)/shard_map/psum | solution.py:35
  137.4 208.5 %all-reduce.11.cloned.1.call-start = ((), (), s32[]{:S(2)}) async-start(), calls=%async_computation.2 | async-start | bytes 786432 | tf_op jit(solution)/shard_map/psum | solution.py:36
  235.7 207.8 %all-reduce.13.cloned.1.call-start = ((), (), s32[]{:S(2)}) async-start(), calls=%async_computation.3 | async-start | bytes 786432 | tf_op jit(solution)/shard_map/psum | solution.py:37
  349.9 211.9 %all-reduce.15.cloned.1.call-start = ((), (), s32[]{:S(2)}) async-start(), calls=%async_computation.4 | async-start | bytes 2097152 | tf_op jit(solution)/shard_map/psum | solution.py:39
  449.7 118.1 %copy-start.1 = (f32[768,128]{0,1:T(8,128)S(1)}, f32[768,128]{0,1:T(8,128)}, u32[]{:S(2)}) copy-start(f32[768,128]{0,1:T(8,128)} %all-reduce.13.cloned.1.call-done) | copy-start | bytes 1179652
  449.7 163.3 %all-reduce.17.cloned.1.call-start = ((), (), s32[]{:S(2)}) async-start(), calls=%async_computation.5 | async-start | bytes 524288 | tf_op jit(solution)/shard_map/psum | solution.py:41
Sparse Core Ops, SparseCore 0:
  17.2 114.9 all-reduce.6
  137.6 93.4 all-reduce.8
  235.9 109.9 all-reduce.10
  350.0 93.4 all-reduce.12
  449.8 111.9 all-reduce.14
  567.9 45.0 all-reduce.16
where the time goes:
time: 623 us; the launch traced here: 622 us
  waiting for transfers between devices  568 us (91%)
  matrix products  33.6 us (5%)
  between operations  14.2 us (2%)
    psum x1, waiting for transfers between devices, per_device(): forward = lax.psum(jnp.dot(inverse, masked, precision=HIGH), 'col')  114 us
    psum x1, waiting for transfers between devices, per_device(): correction = lax.psum(jnp.dot(couple, picked, precision=HIGH), 'col')  112 us
    psum x1, waiting for transfers between devices, per_device(): root_fwd = lax.psum(jnp.dot(root_inv, update, precision=HIGH), 'col')  110 us
    psum x1, waiting for transfers between devices, per_device(): update = root_rhs - lax.psum(spread, ('front', 'row'))  93.6 us
    psum x1, waiting for transfers between devices, per_device(): root_back = lax.psum(lead_dot(root_inv, root_fwd), ('front', 'row'))  93.4 us
    psum x1, waiting for transfers between devices, per_device(): child_back = col_live * lax.psum(lead_dot(inverse, reduced), 'row')  44.3 us
    dot_general x4, matrix products, lead_dot(): lax.dot_general(left, right, (((0,), (0,)), ((), ())), precision=HIGH)  15.1 us
  transfers between devices with their start and end apart: 6, of which 6 were waited for; matrix products, arithmetic and copies ran while one was open for 0% of the time, Pallas kernels for 0%

commit v1 on v0

v1 whole, which is shorter than its diff:
```python
import jax
import jax.numpy as jnp
from jax import lax
from jax.experimental import pallas as pl
from jax.experimental.pallas import tpu as pltpu
from jax.sharding import PartitionSpec as P

MESH = pl.DeviceIdType.MESH
F32 = jnp.float32
BF16 = jnp.bfloat16
NZ = 8
NXY = 16
BLK = 128
RBLK = 48
SLAB = 8
YSLAB = 32


def split(value):
    high = value.astype(BF16)
    low = (value - high.astype(F32)).astype(BF16)
    return high, low


def stack(value, axis):
    return jnp.concatenate(split(value), axis=axis)


def mm(left, right):
    return jnp.dot(left, right, preferred_element_type=F32)


def fold(value):
    rows, cols = value.shape[0] // 2, value.shape[1] // 2
    return (value[:rows, :cols] + value[:rows, cols:]) + (value[rows:, :cols] + value[rows:, cols:])


def halves(value):
    rows = value.shape[0] // 2
    return value[:rows] + value[rows:]


def far_first(step):
    return 4 + (1 - 2 * (step % 2)) * ((step + 1) // 2)


def plane_step(step):
    at = step + (step + 5) // 15 if isinstance(step, int) else step + (step + 5) // 15
    return (2 + at // 4) % 4, (2 + at % 4) % 4


def kernel(
    rhs_hbm, root_hbm, inv_hbm, cpl_hbm, rinv_hbm, counts, map_ref,
    child_out, root_out,
    rhs_v, root_v, inv_v, cpl_v, rinv_v,
    inv_hi, inv_lo, cpl_hi, cpl_lo, rin_hi, rin_lo,
    vec_hl, place, place_t, root_t,
    part1, core1, rs1, full1,
    part5, core5, rs5, full5,
    spread_s, xyr2, upd_t,
    part3, core3, rs3, full3,
    back_s, xyr4, back_t,
    pick_hl, acc_b, acc_c, own_fwd,
    ypart, yrs, yfull,
    load_sem, out_sem,
    c1s, c1r, z1s, z1r, g1s, g1r, s1s, s1r,
    c5s, c5r, z5s, z5r, g5s, g5r, s5s, s5r,
    c3s, c3r, z3s, z3r, g3s, g3r, s3s, s3r,
    p2s, p2r, q2s, q2r, p4s, p4r, q4s, q4r,
    y6s, y6r, w6s, w6r,
):
    f = lax.axis_index("front")
    r = lax.axis_index("row")
    c = lax.axis_index("col")
    z = c // 2
    k = c % 2
    sib = (f, r, z * 2 + (1 - k))

    def zdev(d):
        return (f, r, ((z + d) % NZ) * 2 + k)

    def xydev(df, dr):
        return ((f + df) % 4, (r + dr) % 4, c)

    def rcopy(src, dst, ss, rs, dev):
        return pltpu.make_async_remote_copy(
            src_ref=src, dst_ref=dst, send_sem=ss, recv_sem=rs, device_id=dev, device_id_type=MESH
        )

    def loop(n, body):
        def step(i, carry):
            body(i)
            return carry

        lax.fori_loop(0, n, step, 0)

    barrier = pltpu.get_barrier_semaphore()
    pl.semaphore_signal(barrier, inc=1, device_id=sib, device_id_type=MESH)
    for d in range(1, NZ):
        pl.semaphore_signal(barrier, inc=1, device_id=zdev(d), device_id_type=MESH)
    for e in range(1, NXY):
        pl.semaphore_signal(barrier, inc=1, device_id=xydev(e // 4, e % 4), device_id_type=MESH)

    def block_of(step):
        half = jnp.where(step < 8, 1 - k, k)
        return half * 8 + (z + far_first(step % 8)) % NZ

    def rows(block, size=BLK):
        return pl.ds(pl.multiple_of(block * size, size), size)

    def inv_load(step):
        at = rows(block_of(step))
        return pltpu.make_async_copy(inv_hbm.at[0, at], inv_v.at[at], load_sem.at[step])

    rhs_load = pltpu.make_async_copy(rhs_hbm.at[0], rhs_v, load_sem.at[16])
    cpl_load = pltpu.make_async_copy(cpl_hbm.at[0], cpl_v, load_sem.at[17])
    rinv_load = pltpu.make_async_copy(rinv_hbm, rinv_v, load_sem.at[18])
    root_load = pltpu.make_async_copy(root_hbm, root_v, load_sem.at[19])
    rhs_load.start()
    loop(16, lambda i: inv_load(i).start())
    cpl_load.start()
    rinv_load.start()
    root_load.start()

    count = counts[f]
    rhs_load.wait()
    spot = c * 512 + lax.broadcasted_iota(jnp.int32, (512, BLK), 0)
    vec_hl[...] = stack(jnp.where(spot < count, rhs_v[...], 0.0), 1)

    own = k * 8 + z

    def reduce_over_col(make, part, core, rs, cs, cr, zs, zr):
        def core_copy(step):
            at = rows(block_of(step))
            return rcopy(part.at[at], core.at[rows((z + far_first(step)) % NZ)], cs.at[step], cr.at[step], sib)

        def z_copy(step):
            at = rows(k * 8 + (z + far_first(step)) % NZ)
            return rcopy(part.at[at], rs.at[step], zs.at[step], zr.at[step], zdev(far_first(step)))

        def other(step):
            at = rows(block_of(step))
            part[at, :] = make(step, at)
            core_copy(step).start()

        def mine(step):
            at = rows(block_of(step + 8))
            value = make(step + 8, at)
            core_copy(step).wait_recv()
            part[at, :] = value + core[rows((z + far_first(step)) % NZ), :]

        def mine_send(step):
            mine(step)
            z_copy(step).start()

        loop(8, other)
        loop(7, mine_send)
        mine(7)

        def finish():
            total = part[rows(own), :]
            for step in range(7):
                z_copy(step).wait_recv()
                total = total + rs[step]
            return total

        def drain():
            loop(8, lambda i: core_copy(i).wait_send())
            loop(7, lambda i: z_copy(i).wait_send())

        return finish, drain

    def gather_over_col(full, size, gs, gr, ss, sr, use):
        def z_copy(step):
            at = rows(own, size)
            return rcopy(full.at[at], full.at[at], gs.at[step], gr.at[step], zdev(far_first(step)))

        def sib_copy(step):
            at = rows(k * 8 + (z + far_first(step)) % NZ, size)
            return rcopy(full.at[at], full.at[at], ss.at[step], sr.at[step], sib)

        def z_arrived(step):
            return (8 - far_first(step)) % NZ

        loop(7, lambda i: z_copy(i).start())
        sib_copy(7).start()
        use(own)

        def mine(i):
            step = 6 - i
            z_copy(step).wait_recv()
            d = z_arrived(step)
            at = rows(k * 8 + (z + d) % NZ, size)
            rcopy(full.at[at], full.at[at], ss.at[step], sr.at[step], sib).start()
            use(k * 8 + (z + d) % NZ)

        loop(7, mine)

        def other(i):
            step = 7 - i
            sib_copy(step).wait_recv()
            use((1 - k) * 8 + (z + z_arrived(step)) % NZ)

        loop(8, other)

        def drain():
            loop(7, lambda i: z_copy(i).wait_send())
            loop(8, lambda i: sib_copy(i).wait_send())

        return drain

    def sum_over_plane(src, recv, full, ps, pr, qs, qr, combine):
        me = f * 4 + r

        def slab(df, dr):
            return pl.ds(pl.multiple_of((((f + df) % 4) * 4 + (r + dr) % 4) * SLAB, SLAB), SLAB)

        def out_copy(step):
            df, dr = plane_step(step)
            return rcopy(src.at[slab(df, dr)], recv.at[step], ps.at[step], pr.at[step], xydev(df, dr))

        mine = pl.ds(pl.multiple_of(me * SLAB, SLAB), SLAB)

        def all_copy(step):
            df, dr = plane_step(step)
            return rcopy(full.at[mine], full.at[mine], qs.at[step], qr.at[step], xydev(df, dr))

        loop(15, lambda i: out_copy(i).start())
        total = src[mine, :]
        for step in range(15):
            out_copy(step).wait_recv()
            total = total + recv[step]
        full[mine, :] = combine(total, mine)
        loop(15, lambda i: all_copy(i).start())
        loop(15, lambda i: all_copy(i).wait_recv())

        def drain():
            loop(15, lambda i: out_copy(i).wait_send())
            loop(15, lambda i: all_copy(i).wait_send())

        return drain

    def make_forward(step, at):
        inv_load(step).wait()
        high, low = split(inv_v[at, :])
        inv_hi[at, :] = high
        inv_lo[at, :] = low
        return fold(mm(jnp.concatenate([high, low], axis=0), vec_hl[...]))

    pl.semaphore_wait(barrier, NZ + NXY - 1)
    finish1, drain1 = reduce_over_col(make_forward, part1, core1, rs1, c1s, c1r, z1s, z1r)

    cpl_load.wait()

    def split_cpl(i):
        at = rows(i)
        high, low = split(cpl_v[at, :])
        cpl_hi[at, :] = high
        cpl_lo[at, :] = low

    loop(16, split_cpl)
    rinv_load.wait()

    def split_rinv(i):
        at = rows(i)
        high, low = split(rinv_v[at, :])
        rin_hi[at, :] = high
        rin_lo[at, :] = low

    loop(6, split_rinv)

    def build_map(i):
        at = rows(i)
        spots = i * BLK + lax.broadcasted_iota(jnp.int32, (BLK, 384), 0)
        hot = (map_ref[...] - c * 768 == spots).astype(F32)
        place[at, :] = hot.astype(BF16)
        place_t[i] = hot.T.astype(BF16)

    loop(6, build_map)
    root_load.wait()
    for i in range(6):
        root_t[:, i * BLK:(i + 1) * BLK] = root_v[i * BLK:(i + 1) * BLK, :].T

    live_at = r * 2048 + own * BLK + lax.broadcasted_iota(jnp.int32, (BLK, BLK), 0)
    forward = jnp.where(live_at < count, finish1(), 0.0)
    own_fwd[...] = forward
    full1[rows(own), :] = forward
    acc_b[...] = jnp.zeros_like(acc_b)

    def use_border(block):
        at = rows(block)
        left = stack(full1[at, :].T, 0)
        acc_b[:, :384] += mm(left, cpl_hi[at, :])
        acc_b[:, 384:] += mm(left, cpl_lo[at, :])

    drain2 = gather_over_col(full1, BLK, g1s, g1r, s1s, s1r, use_border)
    border_hl = stack(fold(acc_b[...]), 0)
    for i in range(6):
        spread_s[:, i * BLK:(i + 1) * BLK] = halves(mm(border_hl, place_t[i]))
    drain3 = sum_over_plane(
        spread_s, xyr2, upd_t, p2s, p2r, q2s, q2r, lambda total, mine: root_t[mine, :] - total
    )

    upd_hl = jnp.concatenate([stack(upd_t[:, i * BLK:(i + 1) * BLK].T, 1) for i in range(6)], axis=0)

    def root_rows(i):
        at = rows(i)
        part3[at, :] = fold(mm(jnp.concatenate([rin_hi[at, :], rin_lo[at, :]], axis=0), upd_hl))

    loop(3, lambda i: root_rows((1 - k) * 3 + i))
    half_other = pl.ds(pl.multiple_of((1 - k) * 384, 384), 384)
    half_mine = pl.ds(pl.multiple_of(k * 384, 384), 384)
    core_copy3 = rcopy(part3.at[half_other], core3, c3s.at[0], c3r.at[0], sib)
    core_copy3.start()
    loop(3, lambda i: root_rows(k * 3 + i))
    core_copy3.wait_recv()
    part3[half_mine, :] += core3[...]

    def z_copy3(step):
        at = rows(k * 8 + (z + far_first(step)) % NZ, RBLK)
        return rcopy(part3.at[at], rs3.at[step], z3s.at[step], z3r.at[step], zdev(far_first(step)))

    loop(7, lambda i: z_copy3(i).start())
    total = part3[rows(own, RBLK), :]
    for step in range(7):
        z_copy3(step).wait_recv()
        total = total + rs3[step]
    full3[rows(own, RBLK), :] = total
    drain4 = gather_over_col(full3, RBLK, g3s, g3r, s3s, s3r, lambda block: None)

    fwd_hl = jnp.concatenate([stack(full3[i * BLK:(i + 1) * BLK, :].T, 0) for i in range(6)], axis=1)
    back_s[...] = halves(mm(fwd_hl, rin_hi[...]) + mm(fwd_hl, rin_lo[...]))
    drain5 = sum_over_plane(back_s, xyr4, back_t, p4s, p4r, q4s, q4r, lambda total, mine: total)
    pick = halves(mm(stack(back_t[...], 0), place[...]))
    for i in range(3):
        pick_hl[i * BLK:(i + 1) * BLK, :] = stack(pick[:, i * BLK:(i + 1) * BLK].T, 1)

    def make_correction(step, at):
        return fold(mm(jnp.concatenate([cpl_hi[at, :], cpl_lo[at, :]], axis=0), pick_hl[...]))

    finish5, drain6 = reduce_over_col(make_correction, part5, core5, rs5, c5s, c5r, z5s, z5r)
    for i in range(6):
        root_v[i * BLK:(i + 1) * BLK, :] = back_t[:, i * BLK:(i + 1) * BLK].T
    root_store = pltpu.make_async_copy(root_v, root_out, out_sem.at[0])
    root_store.start()
    full5[rows(own), :] = jnp.where(live_at < count, own_fwd[...] - finish5(), 0.0)
    acc_c[...] = jnp.zeros_like(acc_c)

    def use_back(block):
        at = rows(block)
        left = stack(full5[at, :].T, 0)
        acc_c[...] += mm(left, inv_hi[at, :]) + mm(left, inv_lo[at, :])

    drain7 = gather_over_col(full5, BLK, g5s, g5r, s5s, s5r, use_back)
    ypart[...] = halves(acc_c[...])

    def yslab(d):
        return pl.ds(pl.multiple_of(((r + d) % 4) * YSLAB, YSLAB), YSLAB)

    def ydev(d):
        return (f, (r + d) % 4, c)

    def y_copy(d):
        return rcopy(ypart.at[yslab(d)], yrs.at[d - 1], y6s.at[d - 1], y6r.at[d - 1], ydev(d))

    def w_copy(d):
        return rcopy(yfull.at[yslab(0)], yfull.at[yslab(0)], w6s.at[d - 1], w6r.at[d - 1], ydev(d))

    for d in (2, 1, 3):
        y_copy(d).start()
    total = ypart[yslab(0), :]
    for d in (1, 3, 2):
        y_copy(d).wait_recv()
        total = total + yrs[d - 1]
    yfull[yslab(0), :] = total
    for d in (2, 1, 3):
        w_copy(d).start()
    for d in (1, 3, 2):
        w_copy(d).wait_recv()
    for i in range(4):
        at = c * 512 + i * BLK + lax.broadcasted_iota(jnp.int32, (BLK, BLK), 0)
        rhs_v[i * BLK:(i + 1) * BLK, :] = jnp.where(at < count, yfull[:, i * BLK:(i + 1) * BLK].T, 0.0)
    child_store = pltpu.make_async_copy(rhs_v, child_out.at[0], out_sem.at[1])
    child_store.start()

    drain1()
    drain2()
    drain3()
    core_copy3.wait_send()
    loop(7, lambda i: z_copy3(i).wait_send())
    drain4()
    drain5()
    drain6()
    drain7()
    for d in (1, 2, 3):
        y_copy(d).wait_send()
        w_copy(d).wait_send()
    root_store.wait()
    child_store.wait()


def per_device(child_rhs, root_rhs, child_inv, coupling, root_inv, pivot_counts, border_map):
    v = pltpu.VMEM
    dma = pltpu.SemaphoreType.DMA
    col_sems = [dma((8,))] * 8
    scratch = [
        v((512, 128), F32), v((768, 128), F32), v((2048, 512), F32), v((2048, 384), F32), v((768, 768), F32),
        v((2048, 512), BF16), v((2048, 512), BF16), v((2048, 384), BF16), v((2048, 384), BF16),
        v((768, 768), BF16), v((768, 768), BF16),
        v((512, 256), BF16), v((768, 384), BF16), v((6, 384, 128), BF16), v((128, 768), F32),
        v((2048, 128), F32), v((1024, 128), F32), v((7, 128, 128), F32), v((2048, 128), F32),
        v((2048, 128), F32), v((1024, 128), F32), v((7, 128, 128), F32), v((2048, 128), F32),
        v((128, 768), F32), v((15, 8, 768), F32), v((128, 768), F32),
        v((768, 128), F32), v((384, 128), F32), v((7, 48, 128), F32), v((768, 128), F32),
        v((128, 768), F32), v((15, 8, 768), F32), v((128, 768), F32),
        v((384, 256), BF16), v((256, 768), F32), v((256, 512), F32), v((128, 128), F32),
        v((128, 512), F32), v((3, 32, 512), F32), v((128, 512), F32),
        dma((20,)), dma((2,)),
    ] + col_sems * 3 + [dma((15,))] * 8 + [dma((3,))] * 4
    hbm = pl.BlockSpec(memory_space=pl.ANY)
    return tuple(
        pl.pallas_call(
            kernel,
            out_shape=(
                jax.ShapeDtypeStruct((1, 512, 128), F32),
                jax.ShapeDtypeStruct((768, 128), F32),
            ),
            in_specs=[hbm] * 5
            + [pl.BlockSpec(memory_space=pltpu.SMEM), pl.BlockSpec(memory_space=pltpu.VMEM)],
            out_specs=(hbm, hbm),
            scratch_shapes=scratch,
            compiler_params=pltpu.CompilerParams(
                collective_id=0, has_side_effects=True, vmem_limit_bytes=56 << 20
            ),
            cost_estimate=pl.CostEstimate(flops=5 * 10**9, bytes_accessed=11 * 10**6, transcendentals=0),
        )(child_rhs, root_rhs, child_inv, coupling, root_inv, pivot_counts, border_map)
    )


def solution(mesh):
    in_specs = (
        P("front", "col", None),
        P("col", None),
        P("front", "row", "col"),
        P("front", "row", "col"),
        P(("front", "row"), "col"),
        P(),
        P("front", "col"),
    )
    out_specs = (P("front", "col", None), P("col", None))
    return jax.shard_map(
        per_device, mesh=mesh, in_specs=in_specs, out_specs=out_specs, check_vma=False
    )
```

time: 623 us -> 146 us (0.23)
  waiting for transfers between devices: 568 us -> 0 us
  Pallas kernels: 0 us -> 142 us
  matrix products: 33.6 us -> 0 us
  between operations: 14.2 us -> 0.64 us
    psum x6 -> x0, waiting for transfers between devices: 568 us -> none  [the longest x1 114 us: per_device(): forward = lax.psum(jnp.dot(inverse, masked, precision=HIGH), 'col')]
    pallas_call x0 -> x1, Pallas kernels: none -> 142 us  [per_device(): pl.pallas_call(kernel, out_shape=(jax.ShapeDtypeStruct((1, 512, 128), F32...]
    dot_general x8 -> x0, matrix products: 33.6 us -> none  [the longest x4 15.1 us: lead_dot(): lax.dot_general(left, right, (((0,), (0,)), ((), ())), precision=HIGH)]
  transfers between devices with their start and end apart: 6 -> 0, of which waited for: 6 -> 0; matrix products, arithmetic and copies ran while one was open for 0% -> 0% of each run, Pallas kernels for 0% -> 0%
where the time goes in v1:
time: 146 us
  Pallas kernels  142 us (97%)
  local copies, waits for them, and re-layouts  3.44 us (2%)
    pallas_call x1, Pallas kernels, per_device(): pl.pallas_call(kernel, out_shape=(jax.ShapeDtypeStruct((1, 512, 128), F32...  142 us
    unnamed x2, local copies, waits for them, and re-layouts  3.44 us

profile of v1, /device:TPU:1, one launch (start us, length us, event | category | flops | bytes accessed | tf_op | source)
XLA Modules:
  0.0 145.6 jit_solution(627674626370292035)
XLA Ops:
  0.6 141.6 %shard_map.86 = (f32[1,512,128]{2,1,0:T(8,128)}, f32[768,128]{1,0:T(8,128)}) custom-call(f32[1,512,128]{2,1,0:T(8,128)} %rhs_hbm.1, f32[768,128]{1,0:T(8,128)} %root_hbm.1, f32[1,2048,512]{2,1,0:T(8,128)} %inv_hbm.1, f32[1,2048,384]{2,1,0:T(8,128)} %cpl_hbm.1, f32[768,768]{1,0:T(8,128)} %rinv_hbm.1, s32[4]{0:T(128)} %counts.1, s32[1,384]{1,0:T(1,128)} %map_ref.1), custom_call_target="tpu_custom_call" | custom-call | flops 5000000000 | bytes 11000000 | tf_op jit(solution)/shard_map/pallas_call | solution.py:422
  142.2 1.7 %copy.11 = f32[1,512,128]{2,1,0:T(8,128)} copy(f32[1,512,128]{2,1,0:T(8,128)} %get-tuple-element.4) | data formatting | bytes 524288
  143.9 1.8 %copy.12 = f32[768,128]{1,0:T(8,128)} copy(f32[768,128]{1,0:T(8,128)} %get-tuple-element.5) | data formatting | bytes 786432

commit v2 on v0

v2 whole, which is shorter than its diff:
```python
import jax
import jax.numpy as jnp
from jax import lax
from jax.experimental import pallas as pl
from jax.experimental.pallas import tpu as pltpu
from jax.sharding import PartitionSpec as P

MESH = pl.DeviceIdType.MESH
F32 = jnp.float32
BF16 = jnp.bfloat16
NZ = 8
NXY = 16
BLK = 128
SRC = 64


def split(value):
    high = value.astype(BF16)
    low = (value - high.astype(F32)).astype(BF16)
    return high, low


def stack(value):
    return jnp.concatenate(split(value), axis=0)


def mm(left, right):
    return jnp.dot(left, right, preferred_element_type=F32)


def nt(left, right):
    return lax.dot_general(left, right, (((1,), (1,)), ((), ())), preferred_element_type=F32)


def halves(value):
    rows = value.shape[0] // 2
    return value[:rows] + value[rows:]


def join(left, right, axis):
    return jnp.concatenate([left, right], axis=axis)


def far_first(step):
    return 4 + (1 - 2 * (step % 2)) * ((step + 1) // 2)


def plane_step(step):
    at = step + (step + 5) // 15
    return (2 + at // 4) % 4, (2 + at % 4) % 4


def gather_offset(at):
    size = jnp.where(at < 1, 0, jnp.where(at < 3, 2, jnp.where(at < 5, 1, jnp.where(at < 7, 3, 4))))
    return size * (1 - 2 * (at % 2))


def loop(n, body):
    def step(i, carry):
        body(i)
        return carry

    lax.fori_loop(0, n, step, 0)


def rows(block, size=BLK):
    return pl.ds(pl.multiple_of(block * size, size), size)


def kernel(
    rhs_hbm, root_hbm, inv_hbm, cpl_hbm, rinv_hbm, counts, map_ref,
    child_out, root_out,
    rhs_v, root_v, inv_v, cpl_v, rinv_v,
    inv_hi, inv_lo, cpl_hi, cpl_lo, rin_hi, rin_lo,
    vec_hl, place, root_t, fwd,
    part1, core1, rs1, full1,
    part5, core5, rs5, full5,
    spread_s, xyr2, upd_t,
    part3, core3, rs3, full3,
    back_s, xyr4, back_t,
    pick_hl, acc_b, acc_c,
    ypart, yrs, yfull,
    load_sem, out_sem,
    c1s, z1s, g1s, p2s, c3s, z3s, g3s, p4s, c5s, z5s, g5s, y6s,
    c1r, z1r, g1r, s1r, c3r, z3r, g3r, s3r, c5r, z5r, g5r, s5r,
    p2r, q2r, p4r, q4r, y6r, w6r,
):
    f = lax.axis_index("front")
    r = lax.axis_index("row")
    c = lax.axis_index("col")
    z = c // 2
    k = c % 2
    sib = (f, r, z * 2 + (1 - k))

    way = 1 - 2 * k

    def chip(d):
        return (z + way * d + 2 * NZ) % NZ

    def zdev(d):
        return (f, r, chip(d) * 2 + k)

    def xydev(df, dr):
        return ((f + df) % 4, (r + dr) % 4, c)

    def rcopy(src, dst, ss, rs, dev):
        return pltpu.make_async_remote_copy(
            src_ref=src, dst_ref=dst, send_sem=ss, recv_sem=rs, device_id=dev, device_id_type=MESH
        )

    def await_blocks(sem, count):
        at = inv_v.at[pl.ds(0, count * 16)]
        pltpu.make_async_copy(at, at, sem).wait()

    def await_slabs(sem, count):
        at = cpl_v.at[pl.ds(0, count * 8)]
        pltpu.make_async_copy(at, at, sem).wait()

    barrier = pltpu.get_barrier_semaphore()
    pl.semaphore_signal(barrier, inc=1, device_id=sib, device_id_type=MESH)
    for d in (-2, -1, 1, 2):
        pl.semaphore_signal(barrier, inc=1, device_id=zdev(d), device_id_type=MESH)
    for e in range(1, NXY):
        pl.semaphore_signal(barrier, inc=1, device_id=xydev(e // 4, e % 4), device_id_type=MESH)

    def zat(step):
        return chip(far_first(step))

    def block_of(step):
        side = jnp.where(step < 8, -1, 1)
        half = jnp.where(step < 8, 1 - k, k)
        return half * 8 + chip(side * far_first(step % 8))

    def zat_other(step):
        return chip(-far_first(step))

    def inv_load(step):
        at = rows(block_of(step))
        return pltpu.make_async_copy(inv_hbm.at[0, at], inv_v.at[at], load_sem.at[step])

    rhs_load = pltpu.make_async_copy(rhs_hbm.at[0], rhs_v, load_sem.at[16])
    cpl_load = pltpu.make_async_copy(cpl_hbm.at[0], cpl_v, load_sem.at[17])
    rinv_load = pltpu.make_async_copy(rinv_hbm, rinv_v, load_sem.at[18])
    root_load = pltpu.make_async_copy(root_hbm, root_v, load_sem.at[19])
    rhs_load.start()
    loop(16, lambda i: inv_load(i).start())
    cpl_load.start()
    rinv_load.start()
    root_load.start()

    count = counts[f]
    own = k * 8 + z
    rhs_load.wait()
    for i in range(4):
        spot = c * 512 + i * BLK + lax.broadcasted_iota(jnp.int32, (BLK, BLK), 1)
        high, low = split(jnp.where(spot < count, rhs_v[i * BLK:(i + 1) * BLK, :].T, 0.0))
        vec_hl[:BLK, i * BLK:(i + 1) * BLK] = high
        vec_hl[BLK:, i * BLK:(i + 1) * BLK] = low


    def pair_at(pair):
        return rows(block_of(2 * pair)), rows(block_of(2 * pair + 1))

    def z_reduce(part, rs, zs, zr):
        def copy(index, src, d):
            return rcopy(src, rs.at[index], zs, zr.at[(0, 0, 1, 2, 2, 2, 2)[index]], zdev(d))

        def send(step):
            index = {0: 0, 1: 1, 2: 2, 5: 3, 6: 4}[step]
            return copy(index, part(zat(step)), {0: 2, 1: 1, 2: -1, 5: 1, 6: -1}[step])

        def arrived(begin, end, sem):
            at = rs.at[pl.ds(begin, end - begin)]
            pltpu.make_async_copy(at, at, zr.at[sem]).wait()

        def relay():
            arrived(0, 2, 0)
            part(chip(2))[...] += rs[0] + rs[1]
            copy(5, part(chip(2)), 2).start()
            arrived(2, 3, 1)
            part(chip(-2))[...] += rs[2]
            copy(6, part(chip(-2)), -2).start()

        def total():
            arrived(3, 7, 2)
            return part(z)[...] + ((rs[3] + rs[4]) + (rs[5] + rs[6]))

        return send, relay, total

    def gather(piece, gs, gr, sr):
        def z_copy(index, d_owner, d):
            at = piece(k, chip(d_owner))
            return rcopy(at, at, gs, gr.at[index], zdev(d))

        def sib_copy(owner):
            at = piece(k, owner)
            return rcopy(at, at, gs, sr.at[owner], sib)

        def sib_arrival(owner):
            at = piece(1 - k, owner)
            return rcopy(at, at, gs, sr.at[owner], sib)

        first = [(0, 0, 2), (1, 0, -2), (2, 0, 1), (3, 0, -1)]
        second = [(4, -2, 1), (5, -2, 2), (6, 2, -1)]
        arrivals = {0: -2, 1: 2, 2: -1, 3: 1, 4: -3, 5: -4, 6: 3}

        def arrive(index):
            z_copy(index, arrivals[index], 1).wait_recv()
            sib_copy(chip(arrivals[index])).start()

        def start():
            for item in first:
                z_copy(*item).start()
            sib_copy(z).start()

        def near():
            arrive(0)
            z_copy(*second[0]).start()
            z_copy(*second[1]).start()
            arrive(1)
            z_copy(*second[2]).start()
            arrive(2)
            arrive(3)

        def far():
            arrive(6)
            arrive(4)
            arrive(5)

        def take(begin, end, use):
            def body(i):
                owner = chip(gather_offset(i + begin))
                sib_arrival(owner).wait_recv()
                use(owner)

            loop(end - begin, body)

        return start, near, far, take


    def slab(p):
        return p % 2, rows(p // 2, 8)

    def plane_at(df, dr):
        return slab(((f + df) % 4) * 4 + (r + dr) % 4)

    here = plane_at(0, 0)

    def plane(src, recv, full, ps, pr, qr):
        def out_copy(step):
            df, dr = plane_step(step)
            return rcopy(src.at[plane_at(df, dr)], recv.at[step], ps, pr, xydev(df, dr))

        def all_copy(step):
            df, dr = plane_step(step)
            return rcopy(full.at[here], full.at[here], ps, qr, xydev(df, dr))

        def start():
            loop(15, lambda i: out_copy(i).start())

        def middle(combine):
            total = src[here]
            pltpu.make_async_copy(recv, recv, pr).wait()
            for step in range(15):
                total = total + recv[step]
            full[here] = combine(total)
            loop(15, lambda i: all_copy(i).start())

        def finish():
            await_slabs(qr, 15)
            return join(full[0], full[1], 1)

        return start, middle, finish


    def forward_pair(pair):
        sides = []
        for step in (2 * pair, 2 * pair + 1):
            inv_load(step).wait()
            at = rows(block_of(step))
            high, low = split(inv_v[at, :])
            inv_hi[at, :] = high
            inv_lo[at, :] = low
            sides.append((high, low))
        (high1, low1), (high2, low2) = sides
        value = halves(nt(vec_hl[...], join(high1, high2, 0)) + nt(vec_hl[...], join(low1, low2, 0)))
        return value[:, :BLK], value[:, BLK:]

    def core_copy1(step):
        return rcopy(part1.at[block_of(step)], core1.at[zat_other(step)], c1s, c1r.at[step], sib)

    def other1(pair):
        first, second = forward_pair(pair)
        part1[block_of(2 * pair)] = first
        part1[block_of(2 * pair + 1)] = second

    loop(4, other1)
    pl.semaphore_wait(barrier, NXY + 4)
    loop(8, lambda i: core_copy1(i).start())

    src_rows = [pl.ds(0, SRC), pl.ds(SRC, SRC)]
    sum1 = [
        z_reduce(lambda owner, h=h: part1.at[k * 8 + owner, src_rows[h]], rs1.at[h], z1s, z1r.at[h])
        for h in range(2)
    ]
    for pair in range(4):
        values = forward_pair(pair + 4)
        for j in range(2):
            step = 2 * pair + j
            core_copy1(step).wait_recv()
            part1[k * 8 + zat(step)] = values[j] + core1[zat(step)]
            if step in (0, 1, 2, 5, 6):
                sum1[0][0](step).start()
    for step in (0, 1, 2, 5, 6):
        sum1[1][0](step).start()

    cpl_load.wait()

    def split_cpl(i):
        at = rows(i)
        high, low = split(cpl_v[at, :])
        cpl_hi[at, :] = high
        cpl_lo[at, :] = low

    loop(16, split_cpl)
    rinv_load.wait()

    def split_rinv(i):
        at = rows(i)
        high, low = split(rinv_v[at, :])
        rin_hi[at, :] = high
        rin_lo[at, :] = low

    loop(6, split_rinv)

    def build_map(i):
        at = rows(i)
        spots = i * BLK + lax.broadcasted_iota(jnp.int32, (BLK, 384), 0)
        place[at, :] = (map_ref[...] - c * 768 == spots).astype(F32).astype(BF16)

    loop(6, build_map)
    root_load.wait()
    for i in range(6):
        turned = root_v[i * BLK:(i + 1) * BLK, :].T
        for h in range(2):
            root_t[h, i // 3, :, (i % 3) * BLK:(i % 3 + 1) * BLK] = turned[h * SRC:(h + 1) * SRC]
    acc_b[...] = jnp.zeros_like(acc_b)
    acc_c[...] = jnp.zeros_like(acc_c)
    live = r * 2048 + own * BLK + lax.broadcasted_iota(jnp.int32, (SRC, BLK), 1) < count

    ag1, xy2, ag3, xy4, ag5 = [], [], [], [], []
    for h in range(2):
        sum1[h][1]()
    for h in range(2):
        forward = jnp.where(live, sum1[h][2](), 0.0)
        fwd[h] = forward
        full1[h, own] = forward
        ag1.append(gather(lambda kk, zz, h=h: full1.at[h, kk * 8 + zz], g1s, g1r.at[h], s1r.at[h]))
        ag1[h][0]()

    def use_border(h):
        def use(owner):
            left = stack(join(full1[h, k * 8 + owner], full1[h, (1 - k) * 8 + owner], 1))
            mine, other = rows(k * 8 + owner), rows((1 - k) * 8 + owner)
            acc_b[h] += mm(left, join(cpl_hi[mine, :], cpl_hi[other, :], 0)) + mm(
                left, join(cpl_lo[mine, :], cpl_lo[other, :], 0)
            )

        return use

    ag1[0][1]()
    ag1[0][3](0, 4, use_border(0))
    ag1[1][1]()
    for h in range(2):
        if h:
            ag1[h][3](0, 4, use_border(h))
        ag1[h][2]()
        ag1[h][3](4, 8, use_border(h))
        border_hl = stack(halves(acc_b[h]))
        for half in range(2):
            spread_s[h, half] = halves(nt(border_hl, place[half * 384:(half + 1) * 384, :]))
        xy2.append(plane(
            spread_s.at[h], xyr2.at[h], upd_t.at[h], p2s, p2r.at[h], q2r.at[h]
        ))
        xy2[h][0]()

    for h in range(2):
        xy2[h][1](lambda total, h=h: root_t.at[h][here] - total)

    def core_copy3(h):
        return rcopy(
            part3.at[h, :, rows(1 - k, 32)], core3.at[h], c3s, c3r.at[h], sib
        )

    def slab3(kk, zz):
        return zz % 2, rows(kk * 4 + zz // 2, 8)

    for h in range(2):
        upd_hl = stack(xy2[h][2]())
        value = halves(nt(upd_hl, rin_hi[...]) + nt(upd_hl, rin_lo[...]))
        part3[h, 0] = value[:, :384]
        part3[h, 1] = value[:, 384:]
        core_copy3(h).start()
    sum3 = []
    for h in range(2):
        core_copy3(h).wait_recv()
        part3[h, :, rows(k, 32)] += core3[h]
        sum3.append(z_reduce(
            lambda owner, h=h: part3.at[h].at[slab3(k, owner)], rs3.at[h], z3s, z3r.at[h]
        ))
        for step in (0, 1, 2, 5, 6):
            sum3[h][0](step).start()
    for h in range(2):
        sum3[h][1]()
    for h in range(2):
        full3.at[h][slab3(k, z)] = sum3[h][2]()
        ag3.append(gather(lambda kk, zz, h=h: full3.at[h].at[slab3(kk, zz)], g3s, g3r.at[h], s3r.at[h]))
        ag3[h][0]()

    for h in range(2):
        ag3[h][1]()
    for h in range(2):
        ag3[h][2]()
        ag3[h][3](0, 8, lambda owner: None)
        fwd_hl = stack(join(full3[h, 0], full3[h, 1], 1))
        value = halves(mm(fwd_hl, rin_hi[...]) + mm(fwd_hl, rin_lo[...]))
        back_s[h, 0] = value[:, :384]
        back_s[h, 1] = value[:, 384:]
        xy4.append(plane(
            back_s.at[h], xyr4.at[h], back_t.at[h], p4s, p4r.at[h], q4r.at[h]
        ))
        xy4[h][0]()
    for h in range(2):
        xy4[h][1](lambda total: total)

    def core_copy5(h, step):
        return rcopy(part5.at[h, block_of(step)], core5.at[h, zat_other(step)], c5s, c5r.at[h, step], sib)

    sum5 = []
    for h in range(2):
        pick_hl[h] = stack(halves(mm(stack(xy4[h][2]()), place[...])))

        def correction_pair(pair, h=h):
            at1, at2 = pair_at(pair)
            left = pick_hl[h]
            value = halves(
                nt(left, join(cpl_hi[at1, :], cpl_hi[at2, :], 0)) + nt(left, join(cpl_lo[at1, :], cpl_lo[at2, :], 0))
            )
            return value[:, :BLK], value[:, BLK:]

        def other5(pair, h=h):
            values = correction_pair(pair)
            for j in range(2):
                part5[h, block_of(2 * pair + j)] = values[j]
                core_copy5(h, 2 * pair + j).start()

        sum5.append(z_reduce(
            lambda owner, h=h: part5.at[h, k * 8 + owner], rs5.at[h], z5s, z5r.at[h]
        ))
        loop(4, other5)
        if h:
            sum5[0][1]()
        for pair in range(4):
            values = correction_pair(pair + 4)
            for j in range(2):
                step = 2 * pair + j
                core_copy5(h, step).wait_recv()
                part5[h, k * 8 + zat(step)] = values[j] + core5[h, zat(step)]
                if step in (0, 1, 2, 5, 6):
                    sum5[h][0](step).start()

    for i in range(6):
        half, at = i // 3, (i % 3) * BLK
        root_v[i * BLK:(i + 1) * BLK, :] = join(back_t[0, half, :, at:at + BLK], back_t[1, half, :, at:at + BLK], 0).T
    root_store = pltpu.make_async_copy(root_v, root_out, out_sem.at[0])
    root_store.start()

    sum5[1][1]()
    for h in range(2):
        full5[h, own] = jnp.where(live, fwd[h] - sum5[h][2](), 0.0)
        ag5.append(gather(lambda kk, zz, h=h: full5.at[h, kk * 8 + zz], g5s, g5r.at[h], s5r.at[h]))
        ag5[h][0]()

    def yslab(d):
        return rows((r + d) % 4, 16)

    def ydev(d):
        return (f, (r + d) % 4, c)

    def y_copy(h, d):
        return rcopy(ypart.at[h, yslab(d)], yrs.at[h, d - 1], y6s, y6r.at[h], ydev(d))

    def w_copy(h, d):
        return rcopy(yfull.at[h, yslab(0)], yfull.at[h, yslab(0)], y6s, w6r.at[h], ydev(d))

    def use_back(h):
        def use(owner):
            left = stack(join(full5[h, k * 8 + owner], full5[h, (1 - k) * 8 + owner], 1))
            mine, other = rows(k * 8 + owner), rows((1 - k) * 8 + owner)
            acc_c[h] += mm(left, join(inv_hi[mine, :], inv_hi[other, :], 0)) + mm(
                left, join(inv_lo[mine, :], inv_lo[other, :], 0)
            )

        return use

    ag5[0][1]()
    ag5[0][3](0, 4, use_back(0))
    ag5[1][1]()
    for h in range(2):
        if h:
            ag5[h][3](0, 4, use_back(h))
        ag5[h][2]()
        ag5[h][3](4, 8, use_back(h))
        ypart[h] = halves(acc_c[h])
        for d in (2, 1, 3):
            y_copy(h, d).start()
    for h in range(2):
        total = ypart[h, yslab(0)]
        pltpu.make_async_copy(yrs.at[h], yrs.at[h], y6r.at[h]).wait()
        for d in (1, 3, 2):
            total = total + yrs[h, d - 1]
        yfull[h, yslab(0)] = total
        for d in (2, 1, 3):
            w_copy(h, d).start()
    for h in range(2):
        await_blocks(w6r.at[h], 3)
    for i in range(4):
        at = c * 512 + i * BLK + lax.broadcasted_iota(jnp.int32, (BLK, BLK), 0)
        value = join(yfull[0, :, i * BLK:(i + 1) * BLK], yfull[1, :, i * BLK:(i + 1) * BLK], 0).T
        rhs_v[i * BLK:(i + 1) * BLK, :] = jnp.where(at < count, value, 0.0)
    child_store = pltpu.make_async_copy(rhs_v, child_out.at[0], out_sem.at[1])
    child_store.start()
    await_blocks(c1s, 8 * 2)
    await_blocks(z1s, 2 * 7)
    await_blocks(g1s, 2 * 15)
    await_slabs(p2s, 2 * 30)
    await_slabs(c3s, 2 * 8)
    await_slabs(z3s, 2 * 7)
    await_slabs(g3s, 2 * 15)
    await_slabs(p4s, 2 * 30)
    await_blocks(c5s, 2 * 8)
    await_blocks(z5s, 2 * 7)
    await_blocks(g5s, 2 * 15)
    await_blocks(y6s, 2 * 6)
    root_store.wait()
    child_store.wait()


def hand_over(child, root, child_out, root_out):
    child_out[...] = child[...]
    root_out[...] = root[...]


def per_device(child_rhs, root_rhs, child_inv, coupling, root_inv, pivot_counts, border_map):
    def v(*shape, dtype=F32):
        return pltpu.VMEM(shape, dtype)

    dma = pltpu.SemaphoreType.DMA
    scratch = [
        v(512, 128), v(768, 128), v(2048, 512), v(2048, 384), v(768, 768),
        v(2048, 512, dtype=BF16), v(2048, 512, dtype=BF16), v(2048, 384, dtype=BF16), v(2048, 384, dtype=BF16),
        v(768, 768, dtype=BF16), v(768, 768, dtype=BF16),
        v(256, 512, dtype=BF16), v(768, 384, dtype=BF16), v(2, 2, 64, 384), v(2, 64, 128),
        v(16, 128, 128), v(8, 128, 128), v(2, 7, 64, 128), v(2, 16, 64, 128),
        v(2, 16, 64, 128), v(2, 8, 64, 128), v(2, 7, 64, 128), v(2, 16, 64, 128),
        v(2, 2, 64, 384), v(2, 15, 8, 384), v(2, 2, 64, 384),
        v(2, 2, 64, 384), v(2, 2, 32, 384), v(2, 7, 8, 384), v(2, 2, 64, 384),
        v(2, 2, 64, 384), v(2, 15, 8, 384), v(2, 2, 64, 384),
        v(2, 128, 384, dtype=BF16), v(2, 128, 384), v(2, 128, 512),
        v(2, 64, 512), v(2, 3, 16, 512), v(2, 64, 512),
        dma((20,)), dma((2,)),
    ]
    scratch += [dma] * 12
    scratch += [dma((8,)), dma((2, 3)), dma((2, 7)), dma((2, 8))]
    scratch += [dma((2,)), dma((2, 3)), dma((2, 7)), dma((2, 8))]
    scratch += [dma((2, 8)), dma((2, 3)), dma((2, 7)), dma((2, 8))]
    scratch += [dma((2,))] * 6
    hbm = pl.BlockSpec(memory_space=pl.ANY)
    results = tuple(
        pl.pallas_call(
            kernel,
            out_shape=(
                jax.ShapeDtypeStruct((1, 512, 128), F32),
                jax.ShapeDtypeStruct((768, 128), F32),
            ),
            in_specs=[hbm] * 5
            + [pl.BlockSpec(memory_space=pltpu.SMEM), pl.BlockSpec(memory_space=pltpu.VMEM)],
            out_specs=(hbm, hbm),
            scratch_shapes=scratch,
            compiler_params=pltpu.CompilerParams(
                collective_id=0, has_side_effects=True, vmem_limit_bytes=56 << 20
            ),
            cost_estimate=pl.CostEstimate(flops=5 * 10**9, bytes_accessed=11 * 10**6, transcendentals=0),
        )(child_rhs, root_rhs, child_inv, coupling, root_inv, pivot_counts, border_map)
    )
    vmem = pl.BlockSpec(memory_space=pltpu.VMEM)
    return tuple(
        pl.pallas_call(
            hand_over,
            out_shape=tuple(jax.ShapeDtypeStruct(a.shape, a.dtype) for a in results),
            in_specs=[vmem] * 2,
            out_specs=(vmem, vmem),
        )(*results)
    )


def solution(mesh):
    in_specs = (
        P("front", "col", None),
        P("col", None),
        P("front", "row", "col"),
        P("front", "row", "col"),
        P(("front", "row"), "col"),
        P(),
        P("front", "col"),
    )
    out_specs = (P("front", "col", None), P("col", None))
    return jax.shard_map(
        per_device, mesh=mesh, in_specs=in_specs, out_specs=out_specs, check_vma=False
    )
```

time: 623 us -> 112 us (0.18)
  waiting for transfers between devices: 568 us -> 0 us
  Pallas kernels: 0 us -> 111 us
  matrix products: 33.6 us -> 0 us
  between operations: 14.2 us -> 0.64 us
    psum x6 -> x0, waiting for transfers between devices: 568 us -> none  [the longest x1 114 us: per_device(): forward = lax.psum(jnp.dot(inverse, masked, precision=HIGH), 'col')]
    pallas_call x0 -> x2, Pallas kernels: none -> 111 us  [the longest x1 109 us: per_device(): pl.pallas_call(kernel, out_shape=(jax.ShapeDtypeStruct((1, 512, 128), F32...]
    dot_general x8 -> x0, matrix products: 33.6 us -> none  [the longest x4 15.1 us: lead_dot(): lax.dot_general(left, right, (((0,), (0,)), ((), ())), precision=HIGH)]
  transfers between devices with their start and end apart: 6 -> 0, of which waited for: 6 -> 0; matrix products, arithmetic and copies ran while one was open for 0% -> 0% of each run, Pallas kernels for 0% -> 0%
where the time goes in v2:
time: 112 us
  Pallas kernels  111 us (99%)
    pallas_call x1, Pallas kernels, per_device(): pl.pallas_call(kernel, out_shape=(jax.ShapeDtypeStruct((1, 512, 128), F32...  109 us

profile of v2, /device:TPU:1, one launch (start us, length us, event | category | flops | bytes accessed | tf_op | source)
XLA Modules:
  0.0 111.8 jit_solution(16382181397617672394)
XLA Ops:
  0.6 109.3 %shard_map.86 = (f32[1,512,128]{2,1,0:T(8,128)}, f32[768,128]{1,0:T(8,128)}) custom-call(f32[1,512,128]{2,1,0:T(8,128)} %rhs_hbm.1, f32[768,128]{1,0:T(8,128)} %root_hbm.1, f32[1,2048,512]{2,1,0:T(8,128)} %inv_hbm.1, f32[1,2048,384]{2,1,0:T(8,128)} %cpl_hbm.1, f32[768,768]{1,0:T(8,128)} %rinv_hbm.1, s32[4]{0:T(128)} %counts.1, s32[1,384]{1,0:T(1,128)} %map_ref.1), custom_call_target="tpu_custom_call" | custom-call | flops 5000000000 | bytes 11000000 | tf_op jit(solution)/shard_map/pallas_call | solution.py:580
  109.9 1.9 %shard_map.87 = (f32[1,512,128]{2,1,0:T(8,128)}, f32[768,128]{1,0:T(8,128)}) custom-call(f32[1,512,128]{2,1,0:T(8,128)} %get-tuple-element.4.child, f32[768,128]{1,0:T(8,128)} %get-tuple-element.5.root), custom_call_target="tpu_custom_call" | custom-call | tf_op jit(solution)/shard_map/pallas_call | solution.py:598

commit v3 on v2

v3 whole, which is shorter than its diff:
```python
import jax
import jax.numpy as jnp
from jax import lax
from jax.experimental import pallas as pl
from jax.experimental.pallas import tpu as pltpu
from jax.sharding import PartitionSpec as P

MESH = pl.DeviceIdType.MESH
F32 = jnp.float32
BF16 = jnp.bfloat16
NZ = 8
NXY = 16
BLK = 128
SRC = 64
ARRIVALS = (0, -2, 2, -1, 1, 3, -3, -4)


def split(value):
    high = value.astype(BF16)
    low = (value - high.astype(F32)).astype(BF16)
    return high, low


def stack(value):
    return jnp.concatenate(split(value), axis=0)


def mm(left, right):
    return jnp.dot(left, right, preferred_element_type=F32)


def halves(value):
    rows = value.shape[0] // 2
    return value[:rows] + value[rows:]


def join(left, right, axis):
    return jnp.concatenate([left, right], axis=axis)


def far_first(step):
    return 4 + (1 - 2 * (step % 2)) * ((step + 1) // 2)


def plane_step(step):
    at = step + (step + 5) // 15
    return (2 + at // 4) % 4, (2 + at % 4) % 4


def loop(n, body):
    def step(i, carry):
        body(i)
        return carry

    lax.fori_loop(0, n, step, 0)


def rows(block, size=BLK):
    return pl.ds(pl.multiple_of(block * size, size), size)


def kernel(
    rhs_hbm, root_hbm, inv_hbm, cpl_hbm, rinv_hbm, counts, map_ref,
    child_out, root_out,
    rhs_v, root_v, inv_v, cpl_v, rinv_v,
    inv_hi, inv_lo, cpl_hi, cpl_lo, rin_hi, rin_lo,
    vec_hl, place, place_t, cplt_hi, cplt_lo, rint_hi, rint_lo, root_t, fwd,
    part1, core1, rs1, full1,
    part5, core5, rs5, full5,
    spread_s, xyr2, upd_t,
    part3, core3, rs3, full3,
    back_s, xyr4, back_t,
    acc_b, acc_c,
    ypart, yrs, yfull,
    load_sem, out_sem,
    c1s, z1s, g1s, p2s, c3s, z3s, g3s, p4s, c5s, z5s, g5s, y6s,
    c1r, z1r, g1r, s1r, c3r, z3r, g3r, s3r, c5r, z5r, g5r, s5r,
    p2r, q2r, p4r, q4r, y6r, w6r,
):
    f = lax.axis_index("front")
    r = lax.axis_index("row")
    c = lax.axis_index("col")
    z = c // 2
    k = c % 2
    sib = (f, r, z * 2 + (1 - k))

    way = 1 - 2 * k

    def chip(d):
        return (z + way * d + 2 * NZ) % NZ

    def zdev(d):
        return (f, r, chip(d) * 2 + k)

    def xydev(df, dr):
        return ((f + df) % 4, (r + dr) % 4, c)

    def rcopy(src, dst, ss, rs, dev):
        return pltpu.make_async_remote_copy(
            src_ref=src, dst_ref=dst, send_sem=ss, recv_sem=rs, device_id=dev, device_id_type=MESH
        )

    def await_blocks(sem, count):
        at = inv_v.at[pl.ds(0, count * 16)]
        pltpu.make_async_copy(at, at, sem).wait()

    def await_slabs(sem, count):
        at = cpl_v.at[pl.ds(0, count * 8)]
        pltpu.make_async_copy(at, at, sem).wait()

    def zat(step):
        return chip(far_first(step))

    def block_of(step):
        return (1 - k) * 8 + step if step < 8 else k * 8 + zat(step - 8)

    def inv_load(part):
        at = rows(jnp.where(k == 0, (part + 4) % 8, part), 256)
        return pltpu.make_async_copy(inv_hbm.at[0, at], inv_v.at[at], load_sem.at[part])

    rhs_load = pltpu.make_async_copy(rhs_hbm.at[0], rhs_v, load_sem.at[8])
    cpl_load = pltpu.make_async_copy(cpl_hbm.at[0], cpl_v, load_sem.at[9])
    rinv_load = pltpu.make_async_copy(rinv_hbm, rinv_v, load_sem.at[10])
    root_load = pltpu.make_async_copy(root_hbm, root_v, load_sem.at[11])
    rhs_load.start()
    for part in range(8):
        inv_load(part).start()
    cpl_load.start()
    rinv_load.start()
    root_load.start()

    barrier = pltpu.get_barrier_semaphore()
    pl.semaphore_signal(barrier, inc=1, device_id=sib, device_id_type=MESH)
    for d in range(1, NZ):
        pl.semaphore_signal(barrier, inc=1, device_id=zdev(d), device_id_type=MESH)
    for e in range(1, NXY):
        pl.semaphore_signal(barrier, inc=1, device_id=xydev(e // 4, e % 4), device_id_type=MESH)


    count = counts[f]
    own = k * 8 + z
    rhs_load.wait()
    spot = c * 512 + lax.broadcasted_iota(jnp.int32, (512, BLK), 0)
    vec_hl[...] = jnp.concatenate(split(jnp.where(spot < count, rhs_v[...], 0.0)), axis=1)


    def z_reduce(part, rs, zs, zr):
        def copy(index, src, d):
            return rcopy(src, rs.at[index], zs, zr.at[(0, 0, 1, 2, 2, 2, 2)[index]], zdev(d))

        def send(step):
            index = {0: 0, 1: 1, 2: 2, 5: 3, 6: 4}[step]
            return copy(index, part(zat(step)), {0: 2, 1: 1, 2: -1, 5: 1, 6: -1}[step])

        def arrived(begin, end, sem):
            at = rs.at[pl.ds(begin, end - begin)]
            pltpu.make_async_copy(at, at, zr.at[sem]).wait()

        def relay():
            arrived(0, 2, 0)
            part(chip(2))[...] += rs[0] + rs[1]
            copy(5, part(chip(2)), 2).start()
            arrived(2, 3, 1)
            part(chip(-2))[...] += rs[2]
            copy(6, part(chip(-2)), -2).start()

        def total():
            arrived(3, 7, 2)
            return part(z)[...] + ((rs[3] + rs[4]) + (rs[5] + rs[6]))

        return send, relay, total

    def gather(piece, gs, gr, sr):
        def z_copy(index, d_owner, d):
            at = piece(k, chip(d_owner))
            return rcopy(at, at, gs, gr.at[index], zdev(d))

        def sib_copy(owner):
            at = piece(k, owner)
            return rcopy(at, at, gs, sr.at[owner], sib)

        def sib_arrival(owner):
            at = piece(1 - k, owner)
            return rcopy(at, at, gs, sr.at[owner], sib)

        first = [(0, 0, 2), (1, 0, -2), (2, 0, 1), (3, 0, -1)]
        second = [(4, -2, 1), (5, -2, 2), (6, 2, -1)]
        arrivals = {0: -2, 1: 2, 2: -1, 3: 1, 4: -3, 5: -4, 6: 3}

        def arrive(index):
            z_copy(index, arrivals[index], 1).wait_recv()

        def pass_on(index):
            sib_copy(chip(arrivals[index])).start()

        def start():
            for item in first:
                z_copy(*item).start()
            sib_copy(z).start()

        def relay():
            arrive(0)
            z_copy(*second[0]).start()
            z_copy(*second[1]).start()
            pass_on(0)
            arrive(1)
            z_copy(*second[2]).start()
            pass_on(1)

        def near():
            for index in (2, 3):
                arrive(index)
                pass_on(index)

        def far():
            for index in (6, 4, 5):
                arrive(index)
                pass_on(index)

        def take(begin, end, use):
            owners = [chip(d) for d in ARRIVALS[begin:end]]
            for owner in owners:
                sib_arrival(owner).wait_recv()
            return use(owners)

        return start, relay, near, far, take

    def z_reduce_direct(part, rs, zs, zr):
        def start():
            for step in range(7):
                rcopy(part(zat(step)), rs.at[step], zs, zr, zdev(far_first(step))).start()

        def total():
            pltpu.make_async_copy(rs, rs, zr).wait()
            value = part(z)[...]
            for step in range(7):
                value = value + rs[step]
            return value

        return start, total

    def gather_direct(piece, gs, gr, sr):
        def z_copy(step, owner):
            at = piece(k, owner)
            return rcopy(at, at, gs, gr.at[step], zdev(far_first(step)))

        def sib_copy(owner):
            at = piece(k, owner)
            return rcopy(at, at, gs, sr, sib)

        def start():
            for step in range(7):
                z_copy(step, z).start()
            sib_copy(z).start()

        def finish():
            for step in (5, 6, 3, 4, 1, 2, 0):
                owner = chip(-far_first(step))
                z_copy(step, owner).wait_recv()
                sib_copy(owner).start()
            await_slabs(sr, NZ)

        return start, finish


    def slab(p):
        return p % 2, rows(p // 2, 8)

    def plane_at(df, dr):
        return slab(((f + df) % 4) * 4 + (r + dr) % 4)

    here = plane_at(0, 0)

    def plane(src, recv, full, ps, pr, qr):
        def out_copy(step):
            df, dr = plane_step(step)
            return rcopy(src.at[plane_at(df, dr)], recv.at[step], ps, pr, xydev(df, dr))

        def all_copy(step):
            df, dr = plane_step(step)
            return rcopy(full.at[here], full.at[here], ps, qr, xydev(df, dr))

        def start():
            for step in range(15):
                out_copy(step).start()

        def middle(combine):
            total = src[here]
            pltpu.make_async_copy(recv, recv, pr).wait()
            for step in range(15):
                total = total + recv[step]
            full[here] = combine(total)
            for step in range(15):
                all_copy(step).start()

        def finish():
            await_slabs(qr, 15)
            return join(full[0], full[1], 1)

        return start, middle, finish


    def forward_group(group):
        steps = range(4 * group, 4 * group + 4)
        for part in ((0, 1), (2, 3), (4, 5, 6, 7), ())[group]:
            inv_load(part).wait()
        highs, lows = [], []
        for step in steps:
            at = rows(block_of(step))
            high, low = split(inv_v[at, :])
            inv_hi[at, :] = high
            inv_lo[at, :] = low
            highs.append(high)
            lows.append(low)
        value = mm(jnp.concatenate(highs + lows, axis=0), vec_hl[...])
        value = halves(value[:, :BLK] + value[:, BLK:])
        return [value[j * BLK:(j + 1) * BLK].T for j in range(4)]

    core_copy1 = rcopy(part1.at[rows(1 - k, 8)], core1, c1s, c1r, sib)

    for group in range(2):
        for j, value in enumerate(forward_group(group)):
            part1[block_of(4 * group + j)] = value
    pl.semaphore_wait(barrier, NZ + NXY - 1)
    core_copy1.start()

    src_rows = [pl.ds(0, SRC), pl.ds(SRC, SRC)]
    sum1 = [
        z_reduce(lambda owner, h=h: part1.at[k * 8 + owner, src_rows[h]], rs1.at[h], z1s, z1r.at[h])
        for h in range(2)
    ]
    for group in range(2):
        values = forward_group(group + 2)
        if not group:
            core_copy1.wait_recv()
        for j in range(4):
            owner = zat(4 * group + j)
            part1[k * 8 + owner] = values[j] + core1[owner]
        for step in ((0, 1, 2), (5, 6))[group]:
            sum1[0][0](step).start()
    for step in (0, 1, 2, 5, 6):
        sum1[1][0](step).start()

    cpl_load.wait()

    def split_cpl(i):
        at = rows(i)
        high, low = split(cpl_v[at, :])
        cpl_hi[at, :] = high
        cpl_lo[at, :] = low

    loop(16, split_cpl)

    def build_map(i):
        at = rows(i)
        spots = i * BLK + lax.broadcasted_iota(jnp.int32, (BLK, 384), 0)
        hot = (map_ref[...] - c * 768 == spots).astype(F32)
        place[at, :] = hot.astype(BF16)
        place_t[i] = hot.T.astype(BF16)

    loop(6, build_map)

    def split_rinv(i):
        at = rows(i)
        value = rinv_v[at, :]
        high, low = split(value)
        rin_hi[at, :] = high
        rin_lo[at, :] = low
        high, low = split(value.T)
        rint_hi[i] = high
        rint_lo[i] = low

    def turn_cpl(i):
        high, low = split(cpl_v[rows(i), :].T)
        cplt_hi[i] = high
        cplt_lo[i] = low

    root_load.wait()
    for i in range(6):
        turned = root_v[i * BLK:(i + 1) * BLK, :].T
        for h in range(2):
            root_t[h, i // 3, :, (i % 3) * BLK:(i % 3 + 1) * BLK] = turned[h * SRC:(h + 1) * SRC]
    live = r * 2048 + own * BLK + lax.broadcasted_iota(jnp.int32, (SRC, BLK), 1) < count

    ag1, xy2, ag3, xy4, ag5 = [], [], [], [], []
    for h in range(2):
        sum1[h][1]()
    rinv_load.wait()
    loop(6, split_rinv)
    for h in range(2):
        forward = jnp.where(live, sum1[h][2](), 0.0)
        fwd[h] = forward
        full1[h, own] = forward
        ag1.append(gather(lambda kk, zz, h=h: full1.at[h, kk * 8 + zz], g1s, g1r.at[h], s1r.at[h]))
        ag1[h][0]()

    def use_border(h):
        def use(owners):
            blocks = [side * 8 + owner for owner in owners for side in (k, 1 - k)]
            left = stack(jnp.concatenate([full1[h, block] for block in blocks], axis=1))
            high = jnp.concatenate([cpl_hi[rows(block), :] for block in blocks], axis=0)
            low = jnp.concatenate([cpl_lo[rows(block), :] for block in blocks], axis=0)
            return mm(left, high) + mm(left, low)

        return use

    for h in range(2):
        ag1[h][1]()
    for h in range(2):
        ag1[h][2]()
    for h in range(2):
        ag1[h][3]()
        acc_b[...] = ag1[h][4](0, 4, use_border(h))
        whole = halves(acc_b[...] + ag1[h][4](4, 8, use_border(h)))
        border_hl = stack(whole)
        spread = halves(mm(border_hl, jnp.concatenate([place_t[i] for i in range(6)], axis=1)))
        spread_s[h, 0] = spread[:, :384]
        spread_s[h, 1] = spread[:, 384:]
        xy2.append(plane(
            spread_s.at[h], xyr2.at[h], upd_t.at[h], p2s, p2r.at[h], q2r.at[h]
        ))
        xy2[h][0]()

    loop(8, turn_cpl)
    for h in range(2):
        xy2[h][1](lambda total, h=h: root_t.at[h][here] - total)

    def core_copy3(h):
        return rcopy(
            part3.at[h, :, rows(1 - k, 32)], core3.at[h], c3s, c3r.at[h], sib
        )

    def slab3(kk, zz):
        return zz % 2, rows(kk * 4 + zz // 2, 8)

    loop(8, lambda i: turn_cpl(i + 8))
    sum3 = []
    for h in range(2):
        upd_hl = stack(xy2[h][2]())
        value = halves(
            mm(upd_hl, jnp.concatenate([rint_hi[i] for i in range(6)], axis=1))
            + mm(upd_hl, jnp.concatenate([rint_lo[i] for i in range(6)], axis=1))
        )
        part3[h, 0] = value[:, :384]
        part3[h, 1] = value[:, 384:]
        core_copy3(h).start()
        core_copy3(h).wait_recv()
        part3[h, :, rows(k, 32)] += core3[h]
        sum3.append(z_reduce_direct(
            lambda owner, h=h: part3.at[h].at[slab3(k, owner)], rs3.at[h], z3s, z3r.at[h]
        ))
        sum3[h][0]()
    for h in range(2):
        full3.at[h][slab3(k, z)] = sum3[h][1]()
        ag3.append(gather_direct(
            lambda kk, zz, h=h: full3.at[h].at[slab3(kk, zz)], g3s, g3r.at[h], s3r.at[h]
        ))
        ag3[h][0]()

    for h in range(2):
        ag3[h][1]()
        fwd_hl = stack(join(full3[h, 0], full3[h, 1], 1))
        value = halves(mm(fwd_hl, rin_hi[...]) + mm(fwd_hl, rin_lo[...]))
        back_s[h, 0] = value[:, :384]
        back_s[h, 1] = value[:, 384:]
        xy4.append(plane(
            back_s.at[h], xyr4.at[h], back_t.at[h], p4s, p4r.at[h], q4r.at[h]
        ))
        xy4[h][0]()
    for h in range(2):
        xy4[h][1](lambda total: total)

    def core_copy5(h, group):
        src = part5.at[h, rows(2 * (1 - k) + group, 4)]
        return rcopy(src, core5.at[h, pl.ds(4 * group, 4)], c5s, c5r.at[h], sib)

    sum5 = []
    for h in range(2):
        back = xy4[h][2]()
        left = stack(halves(mm(stack(back), place[...])))

        def correction_group(group, left=left):
            blocks = [block_of(step) for step in range(4 * group, 4 * group + 4)]
            value = halves(
                mm(left, jnp.concatenate([cplt_hi[block] for block in blocks], axis=1))
                + mm(left, jnp.concatenate([cplt_lo[block] for block in blocks], axis=1))
            )
            return [value[:, j * BLK:(j + 1) * BLK] for j in range(4)]

        for group in range(2):
            for j, value in enumerate(correction_group(group)):
                part5[h, block_of(4 * group + j)] = value
            core_copy5(h, group).start()
        sum5.append(z_reduce(
            lambda owner, h=h: part5.at[h, k * 8 + owner], rs5.at[h], z5s, z5r.at[h]
        ))
        values = correction_group(2) + correction_group(3)
        for step in range(8):
            part5[h, block_of(step + 8)] = values[step]
        pltpu.make_async_copy(core5.at[h], core5.at[h], c5r.at[h]).wait()
        for step in range(8):
            owner = zat(step)
            part5[h, k * 8 + owner] += core5[h, owner]
            if step in (0, 1, 2, 5, 6):
                sum5[h][0](step).start()

    for i in range(6):
        half, at = i // 3, (i % 3) * BLK
        root_v[i * BLK:(i + 1) * BLK, :] = join(back_t[0, half, :, at:at + BLK], back_t[1, half, :, at:at + BLK], 0).T
    root_store = pltpu.make_async_copy(root_v, root_out, out_sem.at[0])
    root_store.start()

    for h in range(2):
        sum5[h][1]()
    for h in range(2):
        full5[h, own] = jnp.where(live, fwd[h] - sum5[h][2](), 0.0)
        ag5.append(gather(lambda kk, zz, h=h: full5.at[h, kk * 8 + zz], g5s, g5r.at[h], s5r.at[h]))
        ag5[h][0]()

    def yslab(d):
        return rows((r + d) % 4, 16)

    def ydev(d):
        return (f, (r + d) % 4, c)

    def y_copy(h, d):
        return rcopy(ypart.at[h, yslab(d)], yrs.at[h, d - 1], y6s, y6r.at[h], ydev(d))

    def w_copy(h, d):
        return rcopy(yfull.at[h, yslab(0)], yfull.at[h, yslab(0)], y6s, w6r.at[h], ydev(d))

    def use_back(h):
        def use(owners):
            blocks = [side * 8 + owner for owner in owners for side in (k, 1 - k)]
            left = stack(jnp.concatenate([full5[h, block] for block in blocks], axis=1))
            high = jnp.concatenate([inv_hi[rows(block), :] for block in blocks], axis=0)
            low = jnp.concatenate([inv_lo[rows(block), :] for block in blocks], axis=0)
            return mm(left, high) + mm(left, low)

        return use

    for h in range(2):
        ag5[h][1]()
    for h in range(2):
        ag5[h][2]()
    for h in range(2):
        ag5[h][3]()
        acc_c[...] = ag5[h][4](0, 4, use_back(h))
        whole = halves(acc_c[...] + ag5[h][4](4, 8, use_back(h)))
        ypart[h] = whole
        for d in (2, 1, 3):
            y_copy(h, d).start()
    for h in range(2):
        total = ypart[h, yslab(0)]
        pltpu.make_async_copy(yrs.at[h], yrs.at[h], y6r.at[h]).wait()
        for d in (1, 3, 2):
            total = total + yrs[h, d - 1]
        yfull[h, yslab(0)] = total
        for d in (2, 1, 3):
            w_copy(h, d).start()
    for h in range(2):
        await_blocks(w6r.at[h], 3)
    for i in range(4):
        at = c * 512 + i * BLK + lax.broadcasted_iota(jnp.int32, (BLK, BLK), 0)
        value = join(yfull[0, :, i * BLK:(i + 1) * BLK], yfull[1, :, i * BLK:(i + 1) * BLK], 0).T
        rhs_v[i * BLK:(i + 1) * BLK, :] = jnp.where(at < count, value, 0.0)
    child_store = pltpu.make_async_copy(rhs_v, child_out.at[0], out_sem.at[1])
    child_store.start()
    await_blocks(c1s, 8 * 2)
    await_blocks(z1s, 2 * 7)
    await_blocks(g1s, 2 * 15)
    await_slabs(p2s, 2 * 30)
    await_slabs(c3s, 2 * 8)
    await_slabs(z3s, 2 * 7)
    await_slabs(g3s, 2 * 15)
    await_slabs(p4s, 2 * 30)
    await_blocks(c5s, 2 * 8)
    await_blocks(z5s, 2 * 7)
    await_blocks(g5s, 2 * 15)
    await_blocks(y6s, 2 * 6)
    root_store.wait()
    child_store.wait()


def hand_over(child, root, child_out, root_out, child_v, root_v, sems):
    loads = [
        pltpu.make_async_copy(child, child_v, sems.at[0]),
        pltpu.make_async_copy(root, root_v, sems.at[1]),
    ]
    stores = [
        pltpu.make_async_copy(child_v, child_out, sems.at[2]),
        pltpu.make_async_copy(root_v, root_out, sems.at[3]),
    ]
    for load in loads:
        load.start()
    for load, store in zip(loads, stores):
        load.wait()
        store.start()
    for store in stores:
        store.wait()


def per_device(child_rhs, root_rhs, child_inv, coupling, root_inv, pivot_counts, border_map):
    def v(*shape, dtype=F32):
        return pltpu.VMEM(shape, dtype)

    dma = pltpu.SemaphoreType.DMA
    scratch = [
        v(512, 128), v(768, 128), v(2048, 512), v(2048, 384), v(768, 768),
        v(2048, 512, dtype=BF16), v(2048, 512, dtype=BF16), v(2048, 384, dtype=BF16), v(2048, 384, dtype=BF16),
        v(768, 768, dtype=BF16), v(768, 768, dtype=BF16),
        v(512, 256, dtype=BF16), v(768, 384, dtype=BF16), v(6, 384, 128, dtype=BF16),
        v(16, 384, 128, dtype=BF16), v(16, 384, 128, dtype=BF16),
        v(6, 768, 128, dtype=BF16), v(6, 768, 128, dtype=BF16), v(2, 2, 64, 384), v(2, 64, 128),
        v(16, 128, 128), v(8, 128, 128), v(2, 7, 64, 128), v(2, 16, 64, 128),
        v(2, 16, 64, 128), v(2, 8, 64, 128), v(2, 7, 64, 128), v(2, 16, 64, 128),
        v(2, 2, 64, 384), v(2, 15, 8, 384), v(2, 2, 64, 384),
        v(2, 2, 64, 384), v(2, 2, 32, 384), v(2, 7, 8, 384), v(2, 2, 64, 384),
        v(2, 2, 64, 384), v(2, 15, 8, 384), v(2, 2, 64, 384),
        v(128, 384), v(128, 512),
        v(2, 64, 512), v(2, 3, 16, 512), v(2, 64, 512),
        dma((12,)), dma((2,)),
    ]
    scratch += [dma] * 12
    scratch += [dma, dma((2, 3)), dma((2, 7)), dma((2, 8))]
    scratch += [dma((2,)), dma((2,)), dma((2, 7)), dma((2,))]
    scratch += [dma((2,)), dma((2, 3)), dma((2, 7)), dma((2, 8))]
    scratch += [dma((2,))] * 6
    hbm = pl.BlockSpec(memory_space=pl.ANY)
    results = tuple(
        pl.pallas_call(
            kernel,
            out_shape=(
                jax.ShapeDtypeStruct((1, 512, 128), F32),
                jax.ShapeDtypeStruct((768, 128), F32),
            ),
            in_specs=[hbm] * 5
            + [pl.BlockSpec(memory_space=pltpu.SMEM), pl.BlockSpec(memory_space=pltpu.VMEM)],
            out_specs=(hbm, hbm),
            scratch_shapes=scratch,
            compiler_params=pltpu.CompilerParams(
                collective_id=0, has_side_effects=True, vmem_limit_bytes=56 << 20
            ),
            cost_estimate=pl.CostEstimate(flops=5 * 10**9, bytes_accessed=11 * 10**6, transcendentals=0),
        )(child_rhs, root_rhs, child_inv, coupling, root_inv, pivot_counts, border_map)
    )
    return tuple(
        pl.pallas_call(
            hand_over,
            out_shape=tuple(jax.ShapeDtypeStruct(a.shape, a.dtype) for a in results),
            in_specs=[hbm] * 2,
            out_specs=(hbm, hbm),
            scratch_shapes=[v(1, 512, 128), v(768, 128), dma((4,))],
            compiler_params=pltpu.CompilerParams(vmem_limit_bytes=56 << 20),
        )(*results)
    )


def solution(mesh):
    in_specs = (
        P("front", "col", None),
        P("col", None),
        P("front", "row", "col"),
        P("front", "row", "col"),
        P(("front", "row"), "col"),
        P(),
        P("front", "col"),
    )
    out_specs = (P("front", "col", None), P("col", None))
    return jax.shard_map(
        per_device, mesh=mesh, in_specs=in_specs, out_specs=out_specs, check_vma=False
    )
```

time: 112 us -> 103 us (0.920)
  Pallas kernels: 111 us -> 102 us
    pallas_call x1, Pallas kernels: 109 us -> 100 us  [per_device(): pl.pallas_call(kernel, out_shape=(jax.ShapeDtypeStruct((1, 512, 128), F32...]
where the time goes in v3:
time: 103 us
  Pallas kernels  102 us (99%)
    pallas_call x1, Pallas kernels, per_device(): pl.pallas_call(kernel, out_shape=(jax.ShapeDtypeStruct((1, 512, 128), F32...  100 us

profile of v3, /device:TPU:1, one launch (start us, length us, event | category | flops | bytes accessed | tf_op | source)
XLA Modules:
  0.0 102.6 jit_solution(8210843166349472878)
XLA Ops:
  0.6 100.1 %shard_map.86 = (f32[1,512,128]{2,1,0:T(8,128)}, f32[768,128]{1,0:T(8,128)}) custom-call(f32[1,512,128]{2,1,0:T(8,128)} %rhs_hbm.1, f32[768,128]{1,0:T(8,128)} %root_hbm.1, f32[1,2048,512]{2,1,0:T(8,128)} %inv_hbm.1, f32[1,2048,384]{2,1,0:T(8,128)} %cpl_hbm.1, f32[768,768]{1,0:T(8,128)} %rinv_hbm.1, s32[4]{0:T(128)} %counts.1, s32[1,384]{1,0:T(1,128)} %map_ref.1), custom_call_target="tpu_custom_call" | custom-call | flops 5000000000 | bytes 11000000 | tf_op jit(solution)/shard_map/pallas_call | solution.py:631
  100.7 1.9 %shard_map.87 = (f32[1,512,128]{2,1,0:T(8,128)}, f32[768,128]{1,0:T(8,128)}) custom-call(f32[1,512,128]{2,1,0:T(8,128)} %get-tuple-element.4.child, f32[768,128]{1,0:T(8,128)} %get-tuple-element.5.root), custom_call_target="tpu_custom_call" | custom-call | tf_op jit(solution)/shard_map/pallas_call | solution.py:648

commit v4 on v3

--- a/solution.py
+++ b/solution.py
@@ -12,6 +12,10 @@
 NXY = 16
 BLK = 128
 SRC = 64
+PLANE = (
+    (2, 2), (2, 1), (2, 3), (1, 2), (3, 2), (2, 0), (0, 2), (1, 1),
+    (3, 3), (1, 3), (3, 1), (0, 1), (0, 3), (1, 0), (3, 0),
+)
 ARRIVALS = (0, -2, 2, -1, 1, 3, -3, -4)
 
 
@@ -29,6 +33,10 @@
     return jnp.dot(left, right, preferred_element_type=F32)
 
 
+def mm_split(left, high, low):
+    return mm(jnp.concatenate([left, left], axis=1), jnp.concatenate([high, low], axis=0))
+
+
 def halves(value):
     rows = value.shape[0] // 2
     return value[:rows] + value[rows:]
@@ -40,11 +48,6 @@
 
 def far_first(step):
     return 4 + (1 - 2 * (step % 2)) * ((step + 1) // 2)
-
-
-def plane_step(step):
-    at = step + (step + 5) // 15
-    return (2 + at // 4) % 4, (2 + at % 4) % 4
 
 
 def loop(n, body):
@@ -60,7 +63,7 @@
 
 
 def kernel(
-    rhs_hbm, root_hbm, inv_hbm, cpl_hbm, rinv_hbm, counts, map_ref,
+    rhs_hbm, root_hbm, inv_hbm, cpl_hbm, rinv_hbm, counts_hbm, map_hbm,
     child_out, root_out,
     rhs_v, root_v, inv_v, cpl_v, rinv_v,
     inv_hi, inv_lo, cpl_hi, cpl_lo, rin_hi, rin_lo,
@@ -72,7 +75,7 @@
     back_s, xyr4, back_t,
     acc_b, acc_c,
     ypart, yrs, yfull,
-    load_sem, out_sem,
+    counts, map_ref, load_sem, out_sem,
     c1s, z1s, g1s, p2s, c3s, z3s, g3s, p4s, c5s, z5s, g5s, y6s,
     c1r, z1r, g1r, s1r, c3r, z3r, g3r, s3r, c5r, z5r, g5r, s5r,
     p2r, q2r, p4r, q4r, y6r, w6r,
@@ -122,9 +125,13 @@
     cpl_load = pltpu.make_async_copy(cpl_hbm.at[0], cpl_v, load_sem.at[9])
     rinv_load = pltpu.make_async_copy(rinv_hbm, rinv_v, load_sem.at[10])
     root_load = pltpu.make_async_copy(root_hbm, root_v, load_sem.at[11])
+    counts_load = pltpu.make_async_copy(counts_hbm, counts, load_sem.at[12])
+    map_load = pltpu.make_async_copy(map_hbm, map_ref, load_sem.at[13])
+    counts_load.start()
     rhs_load.start()
     for part in range(8):
         inv_load(part).start()
+    map_load.start()
     cpl_load.start()
     rinv_load.start()
     root_load.start()
@@ -137,11 +144,14 @@
         pl.semaphore_signal(barrier, inc=1, device_id=xydev(e // 4, e % 4), device_id_type=MESH)
 
 
+    counts_load.wait()
     count = counts[f]
     own = k * 8 + z
     rhs_load.wait()
     spot = c * 512 + lax.broadcasted_iota(jnp.int32, (512, BLK), 0)
-    vec_hl[...] = jnp.concatenate(split(jnp.where(spot < count, rhs_v[...], 0.0)), axis=1)
+    vector = jnp.concatenate(split(jnp.where(spot < count, rhs_v[...], 0.0)), axis=1)
+    vec_hl[:512, :] = vector
+    vec_hl[512:, :] = vector
 
 
     def z_reduce(part, rs, zs, zr):
@@ -273,11 +283,11 @@
 
     def plane(src, recv, full, ps, pr, qr):
         def out_copy(step):
-            df, dr = plane_step(step)
+            df, dr = PLANE[step]
             return rcopy(src.at[plane_at(df, dr)], recv.at[step], ps, pr, xydev(df, dr))
 
         def all_copy(step):
-            df, dr = plane_step(step)
+            df, dr = PLANE[step]
             return rcopy(full.at[here], full.at[here], ps, qr, xydev(df, dr))
 
         def start():
@@ -308,13 +318,13 @@
         for step in steps:
             at = rows(block_of(step))
             high, low = split(inv_v[at, :])
-            inv_hi[at, :] = high
-            inv_lo[at, :] = low
             highs.append(high)
             lows.append(low)
-        value = mm(jnp.concatenate(highs + lows, axis=0), vec_hl[...])
-        value = halves(value[:, :BLK] + value[:, BLK:])
-        return [value[j * BLK:(j + 1) * BLK].T for j in range(4)]
+        values = []
+        for high, low in zip(highs, lows):
+            value = mm(join(high, low, 1), vec_hl[...])
+            values.append((value[:, :BLK] + value[:, BLK:]).T)
+        return values
 
     core_copy1 = rcopy(part1.at[rows(1 - k, 8)], core1, c1s, c1r, sib)
 
@@ -358,6 +368,7 @@
         place[at, :] = hot.astype(BF16)
         place_t[i] = hot.T.astype(BF16)
 
+    map_load.wait()
     loop(6, build_map)
 
     def split_rinv(i):
@@ -370,6 +381,12 @@
         rint_hi[i] = high
         rint_lo[i] = low
 
+    def split_inv(i):
+        at = rows(i)
+        high, low = split(inv_v[at, :])
+        inv_hi[at, :] = high
+        inv_lo[at, :] = low
+
     def turn_cpl(i):
         high, low = split(cpl_v[rows(i), :].T)
         cplt_hi[i] = high
@@ -400,7 +417,7 @@
             left = stack(jnp.concatenate([full1[h, block] for block in blocks], axis=1))
             high = jnp.concatenate([cpl_hi[rows(block), :] for block in blocks], axis=0)
             low = jnp.concatenate([cpl_lo[rows(block), :] for block in blocks], axis=0)
-            return mm(left, high) + mm(left, low)
+            return mm_split(left, high, low)
 
         return use
 
@@ -427,29 +444,34 @@
 
     def core_copy3(h):
         return rcopy(
-            part3.at[h, :, rows(1 - k, 32)], core3.at[h], c3s, c3r.at[h], sib
+            part3.at[h, 1 - k], core3.at[h], c3s, c3r.at[h], sib
         )
 
     def slab3(kk, zz):
-        return zz % 2, rows(kk * 4 + zz // 2, 8)
+        return kk, rows(zz, 8)
 
     loop(8, lambda i: turn_cpl(i + 8))
     sum3 = []
     for h in range(2):
         upd_hl = stack(xy2[h][2]())
-        value = halves(
-            mm(upd_hl, jnp.concatenate([rint_hi[i] for i in range(6)], axis=1))
-            + mm(upd_hl, jnp.concatenate([rint_lo[i] for i in range(6)], axis=1))
-        )
-        part3[h, 0] = value[:, :384]
-        part3[h, 1] = value[:, 384:]
-        core_copy3(h).start()
+        for side in (1 - k, k):
+            blocks = [side * 3 + i for i in range(3)]
+            part3[h, side] = halves(
+                mm_split(
+                    upd_hl,
+                    jnp.concatenate([rint_hi[block] for block in blocks], axis=1),
+                    jnp.concatenate([rint_lo[block] for block in blocks], axis=1),
+                )
+            )
+            if side is not k:
+                core_copy3(h).start()
         core_copy3(h).wait_recv()
-        part3[h, :, rows(k, 32)] += core3[h]
+        part3[h, k] += core3[h]
         sum3.append(z_reduce_direct(
             lambda owner, h=h: part3.at[h].at[slab3(k, owner)], rs3.at[h], z3s, z3r.at[h]
         ))
         sum3[h][0]()
+    loop(16, split_inv)
     for h in range(2):
         full3.at[h][slab3(k, z)] = sum3[h][1]()
         ag3.append(gather_direct(
@@ -460,7 +482,7 @@
     for h in range(2):
         ag3[h][1]()
         fwd_hl = stack(join(full3[h, 0], full3[h, 1], 1))
-        value = halves(mm(fwd_hl, rin_hi[...]) + mm(fwd_hl, rin_lo[...]))
+        value = halves(mm_split(fwd_hl, rin_hi[...], rin_lo[...]))
         back_s[h, 0] = value[:, :384]
         back_s[h, 1] = value[:, 384:]
         xy4.append(plane(
@@ -482,8 +504,11 @@
         def correction_group(group, left=left):
             blocks = [block_of(step) for step in range(4 * group, 4 * group + 4)]
             value = halves(
-                mm(left, jnp.concatenate([cplt_hi[block] for block in blocks], axis=1))
-                + mm(left, jnp.concatenate([cplt_lo[block] for block in blocks], axis=1))
+                mm_split(
+                    left,
+                    jnp.concatenate([cplt_hi[block] for block in blocks], axis=1),
+                    jnp.concatenate([cplt_lo[block] for block in blocks], axis=1),
+                )
             )
             return [value[:, j * BLK:(j + 1) * BLK] for j in range(4)]
 
@@ -535,7 +560,7 @@
             left = stack(jnp.concatenate([full5[h, block] for block in blocks], axis=1))
             high = jnp.concatenate([inv_hi[rows(block), :] for block in blocks], axis=0)
             low = jnp.concatenate([inv_lo[rows(block), :] for block in blocks], axis=0)
-            return mm(left, high) + mm(left, low)
+            return mm_split(left, high, low)
 
         return use
 
@@ -609,17 +634,17 @@
         v(512, 128), v(768, 128), v(2048, 512), v(2048, 384), v(768, 768),
         v(2048, 512, dtype=BF16), v(2048, 512, dtype=BF16), v(2048, 384, dtype=BF16), v(2048, 384, dtype=BF16),
         v(768, 768, dtype=BF16), v(768, 768, dtype=BF16),
-        v(512, 256, dtype=BF16), v(768, 384, dtype=BF16), v(6, 384, 128, dtype=BF16),
+        v(1024, 256, dtype=BF16), v(768, 384, dtype=BF16), v(6, 384, 128, dtype=BF16),
         v(16, 384, 128, dtype=BF16), v(16, 384, 128, dtype=BF16),
         v(6, 768, 128, dtype=BF16), v(6, 768, 128, dtype=BF16), v(2, 2, 64, 384), v(2, 64, 128),
         v(16, 128, 128), v(8, 128, 128), v(2, 7, 64, 128), v(2, 16, 64, 128),
         v(2, 16, 64, 128), v(2, 8, 64, 128), v(2, 7, 64, 128), v(2, 16, 64, 128),
         v(2, 2, 64, 384), v(2, 15, 8, 384), v(2, 2, 64, 384),
-        v(2, 2, 64, 384), v(2, 2, 32, 384), v(2, 7, 8, 384), v(2, 2, 64, 384),
+        v(2, 2, 64, 384), v(2, 64, 384), v(2, 7, 8, 384), v(2, 2, 64, 384),
         v(2, 2, 64, 384), v(2, 15, 8, 384), v(2, 2, 64, 384),
         v(128, 384), v(128, 512),
         v(2, 64, 512), v(2, 3, 16, 512), v(2, 64, 512),
-        dma((12,)), dma((2,)),
+        pltpu.SMEM((4,), jnp.int32), pltpu.VMEM((1, 384), jnp.int32), dma((14,)), dma((2,)),
     ]
     scratch += [dma] * 12
     scratch += [dma, dma((2, 3)), dma((2, 7)), dma((2, 8))]
@@ -634,8 +659,7 @@
                 jax.ShapeDtypeStruct((1, 512, 128), F32),
                 jax.ShapeDtypeStruct((768, 128), F32),
             ),
-            in_specs=[hbm] * 5
-            + [pl.BlockSpec(memory_space=pltpu.SMEM), pl.BlockSpec(memory_space=pltpu.VMEM)],
+            in_specs=[hbm] * 7,
             out_specs=(hbm, hbm),
             scratch_shapes=scratch,
             compiler_params=pltpu.CompilerParams(

time: 103 us -> 99.8 us (0.969)
  Pallas kernels: 102 us -> 99.1 us
    pallas_call x1, Pallas kernels: 100 us -> 97.2 us  [per_device(): pl.pallas_call(kernel, out_shape=(jax.ShapeDtypeStruct((1, 512, 128), F32...]
where the time goes in v4:
time: 99.8 us; the launch traced here: 99.7 us
  Pallas kernels  99.1 us (99%)
    pallas_call x1, Pallas kernels, per_device(): pl.pallas_call(kernel, out_shape=(jax.ShapeDtypeStruct((1, 512, 128), F32...  97.2 us

profile of v4, /device:TPU:1, one launch (start us, length us, event | category | flops | bytes accessed | tf_op | source)
XLA Modules:
  0.0 99.7 jit_solution(10074732493641986774)
XLA Ops:
  0.6 97.2 %shard_map.86 = (f32[1,512,128]{2,1,0:T(8,128)}, f32[768,128]{1,0:T(8,128)}) custom-call(f32[1,512,128]{2,1,0:T(8,128)} %rhs_hbm.1, f32[768,128]{1,0:T(8,128)} %root_hbm.1, f32[1,2048,512]{2,1,0:T(8,128)} %inv_hbm.1, f32[1,2048,384]{2,1,0:T(8,128)} %cpl_hbm.1, f32[768,768]{1,0:T(8,128)} %rinv_hbm.1, s32[4]{0:T(128)} %counts_hbm.1, s32[1,384]{1,0:T(1,128)} %map_hbm.1), custom_call_target="tpu_custom_call" | custom-call | flops 5000000000 | bytes 11000000 | tf_op jit(solution)/shard_map/pallas_call | solution.py:656
  97.9 1.9 %shard_map.87 = (f32[1,512,128]{2,1,0:T(8,128)}, f32[768,128]{1,0:T(8,128)}) custom-call(f32[1,512,128]{2,1,0:T(8,128)} %get-tuple-element.4.child, f32[768,128]{1,0:T(8,128)} %get-tuple-element.5.root), custom_call_target="tpu_custom_call" | custom-call | tf_op jit(solution)/shard_map/pallas_call | solution.py:672

commit v5 on v4

--- a/solution.py
+++ b/solution.py
@@ -12,6 +12,7 @@
 NXY = 16
 BLK = 128
 SRC = 64
+QSRC = 32
 PLANE = (
     (2, 2), (2, 1), (2, 3), (1, 2), (3, 2), (2, 0), (0, 2), (1, 1),
     (3, 3), (1, 3), (3, 1), (0, 1), (0, 3), (1, 0), (3, 0),
@@ -227,11 +228,11 @@
                 arrive(index)
                 pass_on(index)
 
-        def take(begin, end, use):
+        def take(begin, end):
             owners = [chip(d) for d in ARRIVALS[begin:end]]
             for owner in owners:
                 sib_arrival(owner).wait_recv()
-            return use(owners)
+            return owners
 
         return start, relay, near, far, take
 
@@ -334,10 +335,10 @@
     pl.semaphore_wait(barrier, NZ + NXY - 1)
     core_copy1.start()
 
-    src_rows = [pl.ds(0, SRC), pl.ds(SRC, SRC)]
+    quarter = [pl.ds((q % 2) * QSRC, QSRC) for q in range(4)]
     sum1 = [
-        z_reduce(lambda owner, h=h: part1.at[k * 8 + owner, src_rows[h]], rs1.at[h], z1s, z1r.at[h])
-        for h in range(2)
+        z_reduce(lambda owner, q=q: part1.at[k * 8 + owner, pl.ds(q * QSRC, QSRC)], rs1.at[q], z1s, z1r.at[q])
+        for q in range(4)
     ]
     for group in range(2):
         values = forward_group(group + 2)
@@ -347,9 +348,11 @@
             owner = zat(4 * group + j)
             part1[k * 8 + owner] = values[j] + core1[owner]
         for step in ((0, 1, 2), (5, 6))[group]:
-            sum1[0][0](step).start()
+            for q in (0, 1):
+                sum1[q][0](step).start()
     for step in (0, 1, 2, 5, 6):
-        sum1[1][0](step).start()
+        for q in (2, 3):
+            sum1[q][0](step).start()
 
     cpl_load.wait()
 
@@ -397,19 +400,21 @@
         turned = root_v[i * BLK:(i + 1) * BLK, :].T
         for h in range(2):
             root_t[h, i // 3, :, (i % 3) * BLK:(i % 3 + 1) * BLK] = turned[h * SRC:(h + 1) * SRC]
-    live = r * 2048 + own * BLK + lax.broadcasted_iota(jnp.int32, (SRC, BLK), 1) < count
+    live = r * 2048 + own * BLK + lax.broadcasted_iota(jnp.int32, (QSRC, BLK), 1) < count
 
     ag1, xy2, ag3, xy4, ag5 = [], [], [], [], []
-    for h in range(2):
-        sum1[h][1]()
+    for q in range(4):
+        sum1[q][1]()
     rinv_load.wait()
     loop(6, split_rinv)
-    for h in range(2):
-        forward = jnp.where(live, sum1[h][2](), 0.0)
-        fwd[h] = forward
-        full1[h, own] = forward
-        ag1.append(gather(lambda kk, zz, h=h: full1.at[h, kk * 8 + zz], g1s, g1r.at[h], s1r.at[h]))
-        ag1[h][0]()
+    for q in range(4):
+        forward = jnp.where(live, sum1[q][2](), 0.0)
+        fwd[q // 2, quarter[q], :] = forward
+        full1[q // 2, own, quarter[q], :] = forward
+        ag1.append(gather(
+            lambda kk, zz, q=q: full1.at[q // 2, kk * 8 + zz, quarter[q]], g1s, g1r.at[q], s1r.at[q]
+        ))
+        ag1[q][0]()
 
     def use_border(h):
         def use(owners):
@@ -421,14 +426,17 @@
 
         return use
 
-    for h in range(2):
-        ag1[h][1]()
-    for h in range(2):
-        ag1[h][2]()
-    for h in range(2):
-        ag1[h][3]()
-        acc_b[...] = ag1[h][4](0, 4, use_border(h))
-        whole = halves(acc_b[...] + ag1[h][4](4, 8, use_border(h)))
+    for q in range(4):
+        ag1[q][1]()
+    for q in range(4):
+        ag1[q][2]()
+    for h in range(2):
+        for q in (2 * h, 2 * h + 1):
+            ag1[q][3]()
+        owners = [ag1[q][4](0, 4) for q in (2 * h, 2 * h + 1)][0]
+        acc_b[...] = use_border(h)(owners)
+        owners = [ag1[q][4](4, 8) for q in (2 * h, 2 * h + 1)][0]
+        whole = halves(acc_b[...] + use_border(h)(owners))
         border_hl = stack(whole)
         spread = halves(mm(border_hl, jnp.concatenate([place_t[i] for i in range(6)], axis=1)))
         spread_s[h, 0] = spread[:, :384]
@@ -516,9 +524,10 @@
             for j, value in enumerate(correction_group(group)):
                 part5[h, block_of(4 * group + j)] = value
             core_copy5(h, group).start()
-        sum5.append(z_reduce(
-            lambda owner, h=h: part5.at[h, k * 8 + owner], rs5.at[h], z5s, z5r.at[h]
-        ))
+        for q in (2 * h, 2 * h + 1):
+            sum5.append(z_reduce(
+                lambda owner, q=q: part5.at[q // 2, k * 8 + owner, quarter[q]], rs5.at[q], z5s, z5r.at[q]
+            ))
         values = correction_group(2) + correction_group(3)
         for step in range(8):
             part5[h, block_of(step + 8)] = values[step]
@@ -527,7 +536,8 @@
             owner = zat(step)
             part5[h, k * 8 + owner] += core5[h, owner]
             if step in (0, 1, 2, 5, 6):
-                sum5[h][0](step).start()
+                for q in (2 * h, 2 * h + 1):
+                    sum5[q][0](step).start()
 
     for i in range(6):
         half, at = i // 3, (i % 3) * BLK
@@ -535,12 +545,15 @@
     root_store = pltpu.make_async_copy(root_v, root_out, out_sem.at[0])
     root_store.start()
 
-    for h in range(2):
-        sum5[h][1]()
-    for h in range(2):
-        full5[h, own] = jnp.where(live, fwd[h] - sum5[h][2](), 0.0)
-        ag5.append(gather(lambda kk, zz, h=h: full5.at[h, kk * 8 + zz], g5s, g5r.at[h], s5r.at[h]))
-        ag5[h][0]()
+    for q in range(4):
+        sum5[q][1]()
+    for q in range(4):
+        rest = fwd[q // 2, quarter[q], :] - sum5[q][2]()
+        full5[q // 2, own, quarter[q], :] = jnp.where(live, rest, 0.0)
+        ag5.append(gather(
+            lambda kk, zz, q=q: full5.at[q // 2, kk * 8 + zz, quarter[q]], g5s, g5r.at[q], s5r.at[q]
+        ))
+        ag5[q][0]()
 
     def yslab(d):
         return rows((r + d) % 4, 16)
@@ -564,14 +577,17 @@
 
         return use
 
-    for h in range(2):
-        ag5[h][1]()
-    for h in range(2):
-        ag5[h][2]()
-    for h in range(2):
-        ag5[h][3]()
-        acc_c[...] = ag5[h][4](0, 4, use_back(h))
-        whole = halves(acc_c[...] + ag5[h][4](4, 8, use_back(h)))
+    for q in range(4):
+        ag5[q][1]()
+    for q in range(4):
+        ag5[q][2]()
+    for h in range(2):
+        for q in (2 * h, 2 * h + 1):
+            ag5[q][3]()
+        owners = [ag5[q][4](0, 4) for q in (2 * h, 2 * h + 1)][0]
+        acc_c[...] = use_back(h)(owners)
+        owners = [ag5[q][4](4, 8) for q in (2 * h, 2 * h + 1)][0]
+        whole = halves(acc_c[...] + use_back(h)(owners))
         ypart[h] = whole
         for d in (2, 1, 3):
             y_copy(h, d).start()
@@ -637,8 +653,8 @@
         v(1024, 256, dtype=BF16), v(768, 384, dtype=BF16), v(6, 384, 128, dtype=BF16),
         v(16, 384, 128, dtype=BF16), v(16, 384, 128, dtype=BF16),
         v(6, 768, 128, dtype=BF16), v(6, 768, 128, dtype=BF16), v(2, 2, 64, 384), v(2, 64, 128),
-        v(16, 128, 128), v(8, 128, 128), v(2, 7, 64, 128), v(2, 16, 64, 128),
-        v(2, 16, 64, 128), v(2, 8, 64, 128), v(2, 7, 64, 128), v(2, 16, 64, 128),
+        v(16, 128, 128), v(8, 128, 128), v(4, 7, 32, 128), v(2, 16, 64, 128),
+        v(2, 16, 64, 128), v(2, 8, 64, 128), v(4, 7, 32, 128), v(2, 16, 64, 128),
         v(2, 2, 64, 384), v(2, 15, 8, 384), v(2, 2, 64, 384),
         v(2, 2, 64, 384), v(2, 64, 384), v(2, 7, 8, 384), v(2, 2, 64, 384),
         v(2, 2, 64, 384), v(2, 15, 8, 384), v(2, 2, 64, 384),
@@ -647,9 +663,9 @@
         pltpu.SMEM((4,), jnp.int32), pltpu.VMEM((1, 384), jnp.int32), dma((14,)), dma((2,)),
     ]
     scratch += [dma] * 12
-    scratch += [dma, dma((2, 3)), dma((2, 7)), dma((2, 8))]
+    scratch += [dma, dma((4, 3)), dma((4, 7)), dma((4, 8))]
     scratch += [dma((2,)), dma((2,)), dma((2, 7)), dma((2,))]
-    scratch += [dma((2,)), dma((2, 3)), dma((2, 7)), dma((2, 8))]
+    scratch += [dma((2,)), dma((4, 3)), dma((4, 7)), dma((4, 8))]
     scratch += [dma((2,))] * 6
     hbm = pl.BlockSpec(memory_space=pl.ANY)
     results = tuple(

time: 99.8 us -> 99.4 us (level)
  no operation moved by 1% of the time
where the time goes in v5:
time: 99.4 us; the launch traced here: 99.3 us
  Pallas kernels  98.6 us (99%)
    pallas_call x1, Pallas kernels, per_device(): pl.pallas_call(kernel, out_shape=(jax.ShapeDtypeStruct((1, 512, 128), F32...  96.8 us

profile of v5, /device:TPU:1, one launch (start us, length us, event | category | flops | bytes accessed | tf_op | source)
XLA Modules:
  0.0 99.3 jit_solution(14389348082504233359)
XLA Ops:
  0.6 96.8 %shard_map.86 = (f32[1,512,128]{2,1,0:T(8,128)}, f32[768,128]{1,0:T(8,128)}) custom-call(f32[1,512,128]{2,1,0:T(8,128)} %rhs_hbm.1, f32[768,128]{1,0:T(8,128)} %root_hbm.1, f32[1,2048,512]{2,1,0:T(8,128)} %inv_hbm.1, f32[1,2048,384]{2,1,0:T(8,128)} %cpl_hbm.1, f32[768,768]{1,0:T(8,128)} %rinv_hbm.1, s32[4]{0:T(128)} %counts_hbm.1, s32[1,384]{1,0:T(1,128)} %map_hbm.1), custom_call_target="tpu_custom_call" | custom-call | flops 5000000000 | bytes 11000000 | tf_op jit(solution)/shard_map/pallas_call | solution.py:672
  97.4 1.9 %shard_map.87 = (f32[1,512,128]{2,1,0:T(8,128)}, f32[768,128]{1,0:T(8,128)}) custom-call(f32[1,512,128]{2,1,0:T(8,128)} %get-tuple-element.4.child, f32[768,128]{1,0:T(8,128)} %get-tuple-element.5.root), custom_call_target="tpu_custom_call" | custom-call | tf_op jit(solution)/shard_map/pallas_call | solution.py:688

commit v6 on v5

--- a/solution.py
+++ b/solution.py
@@ -77,7 +77,7 @@
     acc_b, acc_c,
     ypart, yrs, yfull,
     counts, map_ref, load_sem, out_sem,
-    c1s, z1s, g1s, p2s, c3s, z3s, g3s, p4s, c5s, z5s, g5s, y6s,
+    sent1, sent3, sent5,
     c1r, z1r, g1r, s1r, c3r, z3r, g3r, s3r, c5r, z5r, g5r, s5r,
     p2r, q2r, p4r, q4r, y6r, w6r,
 ):
@@ -108,6 +108,10 @@
         at = inv_v.at[pl.ds(0, count * 16)]
         pltpu.make_async_copy(at, at, sem).wait()
 
+    def await_quarters(sem, count):
+        at = inv_v.at[pl.ds(0, count * 8)]
+        pltpu.make_async_copy(at, at, sem).wait()
+
     def await_slabs(sem, count):
         at = cpl_v.at[pl.ds(0, count * 8)]
         pltpu.make_async_copy(at, at, sem).wait()
@@ -120,16 +124,18 @@
 
     def inv_load(part):
         at = rows(jnp.where(k == 0, (part + 4) % 8, part), 256)
-        return pltpu.make_async_copy(inv_hbm.at[0, at], inv_v.at[at], load_sem.at[part])
-
-    rhs_load = pltpu.make_async_copy(rhs_hbm.at[0], rhs_v, load_sem.at[8])
-    cpl_load = pltpu.make_async_copy(cpl_hbm.at[0], cpl_v, load_sem.at[9])
-    rinv_load = pltpu.make_async_copy(rinv_hbm, rinv_v, load_sem.at[10])
-    root_load = pltpu.make_async_copy(root_hbm, root_v, load_sem.at[11])
-    counts_load = pltpu.make_async_copy(counts_hbm, counts, load_sem.at[12])
-    map_load = pltpu.make_async_copy(map_hbm, map_ref, load_sem.at[13])
+        return pltpu.make_async_copy(inv_hbm.at[0, at], inv_v.at[at], load_sem.at[(0, 0, 1, 1, 2, 2, 2, 2)[part]])
+
+    rhs_load = pltpu.make_async_copy(rhs_hbm.at[0], rhs_v, load_sem.at[3])
+    cpl_load = pltpu.make_async_copy(cpl_hbm.at[0], cpl_v, load_sem.at[4])
+    rinv_load = pltpu.make_async_copy(rinv_hbm, rinv_v, load_sem.at[5])
+    root_load = pltpu.make_async_copy(root_hbm, root_v, load_sem.at[6])
+    counts_load = pltpu.make_async_copy(counts_hbm, counts, load_sem.at[7])
+    map_load = pltpu.make_async_copy(map_hbm, map_ref, load_sem.at[8])
     counts_load.start()
-    rhs_load.start()
+    for i in range(4):
+        at = pl.ds(i * BLK, BLK)
+        pltpu.make_async_copy(rhs_hbm.at[0, at], rhs_v.at[at], load_sem.at[3]).start()
     for part in range(8):
         inv_load(part).start()
     map_load.start()
@@ -184,15 +190,11 @@
     def gather(piece, gs, gr, sr):
         def z_copy(index, d_owner, d):
             at = piece(k, chip(d_owner))
-            return rcopy(at, at, gs, gr.at[index], zdev(d))
-
-        def sib_copy(owner):
+            return rcopy(at, at, gs, gr.at[(0, 1, 2, 2, 3, 4, 5)[index]], zdev(d))
+
+        def sib_copy(owner, far):
             at = piece(k, owner)
-            return rcopy(at, at, gs, sr.at[owner], sib)
-
-        def sib_arrival(owner):
-            at = piece(1 - k, owner)
-            return rcopy(at, at, gs, sr.at[owner], sib)
+            return rcopy(at, at, gs, sr.at[far], sib)
 
         first = [(0, 0, 2), (1, 0, -2), (2, 0, 1), (3, 0, -1)]
         second = [(4, -2, 1), (5, -2, 2), (6, 2, -1)]
@@ -202,12 +204,12 @@
             z_copy(index, arrivals[index], 1).wait_recv()
 
         def pass_on(index):
-            sib_copy(chip(arrivals[index])).start()
+            sib_copy(chip(arrivals[index]), index // 4).start()
 
         def start():
             for item in first:
                 z_copy(*item).start()
-            sib_copy(z).start()
+            sib_copy(z, 0).start()
 
         def relay():
             arrive(0)
@@ -219,8 +221,8 @@
             pass_on(1)
 
         def near():
+            await_quarters(gr.at[2], 2)
             for index in (2, 3):
-                arrive(index)
                 pass_on(index)
 
         def far():
@@ -228,11 +230,9 @@
                 arrive(index)
                 pass_on(index)
 
-        def take(begin, end):
-            owners = [chip(d) for d in ARRIVALS[begin:end]]
-            for owner in owners:
-                sib_arrival(owner).wait_recv()
-            return owners
+        def take(far):
+            await_quarters(sr.at[far], (5, 3)[far])
+            return [chip(d) for d in (ARRIVALS[:5], ARRIVALS[5:])[far]]
 
         return start, relay, near, far, take
 
@@ -313,8 +313,9 @@
 
     def forward_group(group):
         steps = range(4 * group, 4 * group + 4)
-        for part in ((0, 1), (2, 3), (4, 5, 6, 7), ())[group]:
-            inv_load(part).wait()
+        if group < 3:
+            at = inv_v.at[pl.ds(0, (512, 512, 1024)[group])]
+            pltpu.make_async_copy(at, at, load_sem.at[group]).wait()
         highs, lows = [], []
         for step in steps:
             at = rows(block_of(step))
@@ -327,7 +328,7 @@
             values.append((value[:, :BLK] + value[:, BLK:]).T)
         return values
 
-    core_copy1 = rcopy(part1.at[rows(1 - k, 8)], core1, c1s, c1r, sib)
+    core_copy1 = rcopy(part1.at[rows(1 - k, 8)], core1, sent1, c1r, sib)
 
     for group in range(2):
         for j, value in enumerate(forward_group(group)):
@@ -337,7 +338,7 @@
 
     quarter = [pl.ds((q % 2) * QSRC, QSRC) for q in range(4)]
     sum1 = [
-        z_reduce(lambda owner, q=q: part1.at[k * 8 + owner, pl.ds(q * QSRC, QSRC)], rs1.at[q], z1s, z1r.at[q])
+        z_reduce(lambda owner, q=q: part1.at[k * 8 + owner, pl.ds(q * QSRC, QSRC)], rs1.at[q], sent1, z1r.at[q])
         for q in range(4)
     ]
     for group in range(2):
@@ -412,7 +413,7 @@
         fwd[q // 2, quarter[q], :] = forward
         full1[q // 2, own, quarter[q], :] = forward
         ag1.append(gather(
-            lambda kk, zz, q=q: full1.at[q // 2, kk * 8 + zz, quarter[q]], g1s, g1r.at[q], s1r.at[q]
+            lambda kk, zz, q=q: full1.at[q // 2, kk * 8 + zz, quarter[q]], sent1, g1r.at[q], s1r.at[q]
         ))
         ag1[q][0]()
 
@@ -433,16 +434,16 @@
     for h in range(2):
         for q in (2 * h, 2 * h + 1):
             ag1[q][3]()
-        owners = [ag1[q][4](0, 4) for q in (2 * h, 2 * h + 1)][0]
+        owners = [ag1[q][4](0) for q in (2 * h, 2 * h + 1)][0]
         acc_b[...] = use_border(h)(owners)
-        owners = [ag1[q][4](4, 8) for q in (2 * h, 2 * h + 1)][0]
+        owners = [ag1[q][4](1) for q in (2 * h, 2 * h + 1)][0]
         whole = halves(acc_b[...] + use_border(h)(owners))
         border_hl = stack(whole)
         spread = halves(mm(border_hl, jnp.concatenate([place_t[i] for i in range(6)], axis=1)))
         spread_s[h, 0] = spread[:, :384]
         spread_s[h, 1] = spread[:, 384:]
         xy2.append(plane(
-            spread_s.at[h], xyr2.at[h], upd_t.at[h], p2s, p2r.at[h], q2r.at[h]
+            spread_s.at[h], xyr2.at[h], upd_t.at[h], sent3, p2r.at[h], q2r.at[h]
         ))
         xy2[h][0]()
 
@@ -452,7 +453,7 @@
 
     def core_copy3(h):
         return rcopy(
-            part3.at[h, 1 - k], core3.at[h], c3s, c3r.at[h], sib
+            part3.at[h, 1 - k], core3.at[h], sent3, c3r.at[h], sib
         )
 
     def slab3(kk, zz):
@@ -476,14 +477,14 @@
         core_copy3(h).wait_recv()
         part3[h, k] += core3[h]
         sum3.append(z_reduce_direct(
-            lambda owner, h=h: part3.at[h].at[slab3(k, owner)], rs3.at[h], z3s, z3r.at[h]
+            lambda owner, h=h: part3.at[h].at[slab3(k, owner)], rs3.at[h], sent3, z3r.at[h]
         ))
         sum3[h][0]()
     loop(16, split_inv)
     for h in range(2):
         full3.at[h][slab3(k, z)] = sum3[h][1]()
         ag3.append(gather_direct(
-            lambda kk, zz, h=h: full3.at[h].at[slab3(kk, zz)], g3s, g3r.at[h], s3r.at[h]
+            lambda kk, zz, h=h: full3.at[h].at[slab3(kk, zz)], sent3, g3r.at[h], s3r.at[h]
         ))
         ag3[h][0]()
 
@@ -494,7 +495,7 @@
         back_s[h, 0] = value[:, :384]
         back_s[h, 1] = value[:, 384:]
         xy4.append(plane(
-            back_s.at[h], xyr4.at[h], back_t.at[h], p4s, p4r.at[h], q4r.at[h]
+            back_s.at[h], xyr4.at[h], back_t.at[h], sent3, p4r.at[h], q4r.at[h]
         ))
         xy4[h][0]()
     for h in range(2):
@@ -502,7 +503,7 @@
 
     def core_copy5(h, group):
         src = part5.at[h, rows(2 * (1 - k) + group, 4)]
-        return rcopy(src, core5.at[h, pl.ds(4 * group, 4)], c5s, c5r.at[h], sib)
+        return rcopy(src, core5.at[h, pl.ds(4 * group, 4)], sent5, c5r.at[h], sib)
 
     sum5 = []
     for h in range(2):
@@ -526,7 +527,7 @@
             core_copy5(h, group).start()
         for q in (2 * h, 2 * h + 1):
             sum5.append(z_reduce(
-                lambda owner, q=q: part5.at[q // 2, k * 8 + owner, quarter[q]], rs5.at[q], z5s, z5r.at[q]
+                lambda owner, q=q: part5.at[q // 2, k * 8 + owner, quarter[q]], rs5.at[q], sent5, z5r.at[q]
             ))
         values = correction_group(2) + correction_group(3)
         for step in range(8):
@@ -551,7 +552,7 @@
         rest = fwd[q // 2, quarter[q], :] - sum5[q][2]()
         full5[q // 2, own, quarter[q], :] = jnp.where(live, rest, 0.0)
         ag5.append(gather(
-            lambda kk, zz, q=q: full5.at[q // 2, kk * 8 + zz, quarter[q]], g5s, g5r.at[q], s5r.at[q]
+            lambda kk, zz, q=q: full5.at[q // 2, kk * 8 + zz, quarter[q]], sent5, g5r.at[q], s5r.at[q]
         ))
         ag5[q][0]()
 
@@ -562,10 +563,10 @@
         return (f, (r + d) % 4, c)
 
     def y_copy(h, d):
-        return rcopy(ypart.at[h, yslab(d)], yrs.at[h, d - 1], y6s, y6r.at[h], ydev(d))
+        return rcopy(ypart.at[h, yslab(d)], yrs.at[h, d - 1], sent5, y6r.at[h], ydev(d))
 
     def w_copy(h, d):
-        return rcopy(yfull.at[h, yslab(0)], yfull.at[h, yslab(0)], y6s, w6r.at[h], ydev(d))
+        return rcopy(yfull.at[h, yslab(0)], yfull.at[h, yslab(0)], sent5, w6r.at[h], ydev(d))
 
     def use_back(h):
         def use(owners):
@@ -584,9 +585,9 @@
     for h in range(2):
         for q in (2 * h, 2 * h + 1):
             ag5[q][3]()
-        owners = [ag5[q][4](0, 4) for q in (2 * h, 2 * h + 1)][0]
+        owners = [ag5[q][4](0) for q in (2 * h, 2 * h + 1)][0]
         acc_c[...] = use_back(h)(owners)
-        owners = [ag5[q][4](4, 8) for q in (2 * h, 2 * h + 1)][0]
+        owners = [ag5[q][4](1) for q in (2 * h, 2 * h + 1)][0]
         whole = halves(acc_c[...] + use_back(h)(owners))
         ypart[h] = whole
         for d in (2, 1, 3):
@@ -605,20 +606,12 @@
         at = c * 512 + i * BLK + lax.broadcasted_iota(jnp.int32, (BLK, BLK), 0)
         value = join(yfull[0, :, i * BLK:(i + 1) * BLK], yfull[1, :, i * BLK:(i + 1) * BLK], 0).T
         rhs_v[i * BLK:(i + 1) * BLK, :] = jnp.where(at < count, value, 0.0)
+        part = pl.ds(i * BLK, BLK)
+        pltpu.make_async_copy(rhs_v.at[part], child_out.at[0, part], out_sem.at[1]).start()
     child_store = pltpu.make_async_copy(rhs_v, child_out.at[0], out_sem.at[1])
-    child_store.start()
-    await_blocks(c1s, 8 * 2)
-    await_blocks(z1s, 2 * 7)
-    await_blocks(g1s, 2 * 15)
-    await_slabs(p2s, 2 * 30)
-    await_slabs(c3s, 2 * 8)
-    await_slabs(z3s, 2 * 7)
-    await_slabs(g3s, 2 * 15)
-    await_slabs(p4s, 2 * 30)
-    await_blocks(c5s, 2 * 8)
-    await_blocks(z5s, 2 * 7)
-    await_blocks(g5s, 2 * 15)
-    await_blocks(y6s, 2 * 6)
+    await_blocks(sent1, 8 * 2 + 2 * 7 + 2 * 15)
+    await_slabs(sent3, 2 * 30 + 2 * 8 + 2 * 7 + 2 * 15 + 2 * 30)
+    await_blocks(sent5, 2 * 8 + 2 * 7 + 2 * 15 + 2 * 6)
     root_store.wait()
     child_store.wait()
 
@@ -660,12 +653,12 @@
         v(2, 2, 64, 384), v(2, 15, 8, 384), v(2, 2, 64, 384),
         v(128, 384), v(128, 512),
         v(2, 64, 512), v(2, 3, 16, 512), v(2, 64, 512),
-        pltpu.SMEM((4,), jnp.int32), pltpu.VMEM((1, 384), jnp.int32), dma((14,)), dma((2,)),
+        pltpu.SMEM((4,), jnp.int32), pltpu.VMEM((1, 384), jnp.int32), dma((9,)), dma((2,)),
     ]
-    scratch += [dma] * 12
-    scratch += [dma, dma((4, 3)), dma((4, 7)), dma((4, 8))]
+    scratch += [dma] * 3
+    scratch += [dma, dma((4, 3)), dma((4, 6)), dma((4, 2))]
     scratch += [dma((2,)), dma((2,)), dma((2, 7)), dma((2,))]
-    scratch += [dma((2,)), dma((4, 3)), dma((4, 7)), dma((4, 8))]
+    scratch += [dma((2,)), dma((4, 3)), dma((4, 6)), dma((4, 2))]
     scratch += [dma((2,))] * 6
     hbm = pl.BlockSpec(memory_space=pl.ANY)
     results = tuple(

time: 99.4 us -> 99.3 us (level)
  no operation moved by 1% of the time
where the time goes in v6:
time: 99.3 us; the launch traced here: 99.2 us
  Pallas kernels  98.6 us (99%)
    pallas_call x1, Pallas kernels, per_device(): pl.pallas_call(kernel, out_shape=(jax.ShapeDtypeStruct((1, 512, 128), F32...  96.7 us

profile of v6, /device:TPU:1, one launch (start us, length us, event | category | flops | bytes accessed | tf_op | source)
XLA Modules:
  0.0 99.2 jit_solution(13283460014940463717)
XLA Ops:
  0.6 96.7 %shard_map.86 = (f32[1,512,128]{2,1,0:T(8,128)}, f32[768,128]{1,0:T(8,128)}) custom-call(f32[1,512,128]{2,1,0:T(8,128)} %rhs_hbm.1, f32[768,128]{1,0:T(8,128)} %root_hbm.1, f32[1,2048,512]{2,1,0:T(8,128)} %inv_hbm.1, f32[1,2048,384]{2,1,0:T(8,128)} %cpl_hbm.1, f32[768,768]{1,0:T(8,128)} %rinv_hbm.1, s32[4]{0:T(128)} %counts_hbm.1, s32[1,384]{1,0:T(1,128)} %map_hbm.1), custom_call_target="tpu_custom_call" | custom-call | flops 5000000000 | bytes 11000000 | tf_op jit(solution)/shard_map/pallas_call | solution.py:665
  97.3 1.9 %shard_map.87 = (f32[1,512,128]{2,1,0:T(8,128)}, f32[768,128]{1,0:T(8,128)}) custom-call(f32[1,512,128]{2,1,0:T(8,128)} %get-tuple-element.4.child, f32[768,128]{1,0:T(8,128)} %get-tuple-element.5.root), custom_call_target="tpu_custom_call" | custom-call | tf_op jit(solution)/shard_map/pallas_call | solution.py:681

commit v7 on v6

--- a/solution.py
+++ b/solution.py
@@ -190,7 +190,7 @@
     def gather(piece, gs, gr, sr):
         def z_copy(index, d_owner, d):
             at = piece(k, chip(d_owner))
-            return rcopy(at, at, gs, gr.at[(0, 1, 2, 2, 3, 4, 5)[index]], zdev(d))
+            return rcopy(at, at, gs, gr.at[(0, 1, 2, 2, 3, 3, 3)[index]], zdev(d))
 
         def sib_copy(owner, far):
             at = piece(k, owner)
@@ -226,8 +226,8 @@
                 pass_on(index)
 
         def far():
+            await_quarters(gr.at[3], 3)
             for index in (6, 4, 5):
-                arrive(index)
                 pass_on(index)
 
         def take(far):
@@ -656,9 +656,9 @@
         pltpu.SMEM((4,), jnp.int32), pltpu.VMEM((1, 384), jnp.int32), dma((9,)), dma((2,)),
     ]
     scratch += [dma] * 3
-    scratch += [dma, dma((4, 3)), dma((4, 6)), dma((4, 2))]
+    scratch += [dma, dma((4, 3)), dma((4, 4)), dma((4, 2))]
     scratch += [dma((2,)), dma((2,)), dma((2, 7)), dma((2,))]
-    scratch += [dma((2,)), dma((4, 3)), dma((4, 6)), dma((4, 2))]
+    scratch += [dma((2,)), dma((4, 3)), dma((4, 4)), dma((4, 2))]
     scratch += [dma((2,))] * 6
     hbm = pl.BlockSpec(memory_space=pl.ANY)
     results = tuple(

time: 99.3 us -> 99 us (level)
  no operation moved by 1% of the time
where the time goes in v7:
time: 99 us; the launch traced here: 98.9 us
  Pallas kernels  98.3 us (99%)
    pallas_call x1, Pallas kernels, per_device(): pl.pallas_call(kernel, out_shape=(jax.ShapeDtypeStruct((1, 512, 128), F32...  96.4 us

profile of v7, /device:TPU:1, one launch (start us, length us, event | category | flops | bytes accessed | tf_op | source)
XLA Modules:
  0.0 98.9 jit_solution(13730147760697075127)
XLA Ops:
  0.6 96.4 %shard_map.86 = (f32[1,512,128]{2,1,0:T(8,128)}, f32[768,128]{1,0:T(8,128)}) custom-call(f32[1,512,128]{2,1,0:T(8,128)} %rhs_hbm.1, f32[768,128]{1,0:T(8,128)} %root_hbm.1, f32[1,2048,512]{2,1,0:T(8,128)} %inv_hbm.1, f32[1,2048,384]{2,1,0:T(8,128)} %cpl_hbm.1, f32[768,768]{1,0:T(8,128)} %rinv_hbm.1, s32[4]{0:T(128)} %counts_hbm.1, s32[1,384]{1,0:T(1,128)} %map_hbm.1), custom_call_target="tpu_custom_call" | custom-call | flops 5000000000 | bytes 11000000 | tf_op jit(solution)/shard_map/pallas_call | solution.py:665
  97.0 1.9 %shard_map.87 = (f32[1,512,128]{2,1,0:T(8,128)}, f32[768,128]{1,0:T(8,128)}) custom-call(f32[1,512,128]{2,1,0:T(8,128)} %get-tuple-element.4.child, f32[768,128]{1,0:T(8,128)} %get-tuple-element.5.root), custom_call_target="tpu_custom_call" | custom-call | tf_op jit(solution)/shard_map/pallas_call | solution.py:681
